TPU v7x, 32 devices: a whole 2x2x4 slice. The times are simulated.
32 devices in a mesh: dp: 8 (over z, y), fsdp: 4 (over x, core).
Axes of the slice: x: 2, y: 2, z: 4, core: 2. Of those that a mesh axis runs over, the one named last changes fastest.
Arguments:
- inputs: bfloat16 [32, 784, 384], P(('dp', 'fsdp')), may hold values from -6 to 6
- items: int32 [32, 784], P(('dp', 'fsdp')), may hold values from 0 to 5, never falling along the last dimension, each value on 1 to 320 neighbouring positions
- routes: int32 [2, 32, 784], P(None, ('dp', 'fsdp')), may hold values from 0 to 1, as said below
- slots: int32 [2, 32, 784], P(None, ('dp', 'fsdp')), may hold values from 0 to 255, as said below
- cotangent: bfloat16 [32, 784, 384], P(('dp', 'fsdp')), may hold values from -6 to 6
- params: float32 [2, 2961408], P(None, ('dp', 'fsdp'))
- momentum: float32 [2, 2961408], P(None, ('dp', 'fsdp'))
- average: float32 [2, 2961408], P(None, ('dp', 'fsdp'))
Outputs:
- outputs: bfloat16 [32, 784, 384], P(('dp', 'fsdp'))
- input_grad: float32 [32, 784, 384], P(('dp', 'fsdp'))
- new_params: float32 [2, 2961408], P(None, ('dp', 'fsdp'))
- new_momentum: float32 [2, 2961408], P(None, ('dp', 'fsdp'))
- new_average: float32 [2, 2961408], P(None, ('dp', 'fsdp'))
- vector_grads: float32 [2, 9, 384], replicated
Inputs may be any that keep to these rules, and one draw needn't show every extreme that they name: `routes`: in every half canvas (392 consecutive patches of one canvas) of each block no expert is named by more than 256 patches, and one expert by exactly 256. `slots`: within a half canvas of one block no two patches share both route and slot.
All inputs are finite; a program needn't handle non-finite values.
Results may differ from a plain program's by a relative error of at most 0.02.
The roundings to bfloat16 on the way count: a program that leaves them out, or rounds other values in their place, can miss the bound.
Values may be sent and summed in bfloat16 or wider, within the bound.
No kernel may reach another device: no remote copies, remote signals or barrier semaphores. Data moves between devices by JAX's collectives and lax.ppermute only.
A program may use at most 256 MiB of HBM per device.

v0:
```python
import functools
import math
from typing import Any, NamedTuple

import jax
import jax.numpy as jnp
import numpy as np
from jax import lax
from jax.experimental import pallas as pl
from jax.experimental.pallas import tpu as pltpu
from jax.sharding import PartitionSpec as P

D = 384
HEADS = 12
F = 1536
HEAD_DIM = 32
EXPERTS = 2
CAP = 256
SIDE = 28
WIN = 7
SHIFT = 3
BLOCKS = 2
CELLS = 784
GROUP = 392
RELS = 169
NORM_EPSILON = 1e-05
MOMENTUM_DECAY = 0.9
AVERAGE_DECAY = 0.9
RATE_BASE = 0.1

DP = "dp"
FSDP = "fsdp"
LANES = 128
WROWS = 64
WINDOWS = 16
WTOK = WINDOWS * WROWS
SLOTS = EXPERTS * 2 * CAP
PAIR = 4 * WROWS
QUADS = HEADS // 4
SCALE = HEAD_DIM ** (-0.5)
BF = jnp.bfloat16
F32 = jnp.float32
VMEM_BYTES = 60 * 1024 * 1024


def call(body, out_shape, n_in, scratch=(), aliases=None, smem=0):
    return pl.pallas_call(
        body,
        out_shape=out_shape,
        in_specs=[pl.BlockSpec(memory_space=pltpu.SMEM)] * smem
        + [pl.BlockSpec(memory_space=pltpu.VMEM)] * (n_in - smem),
        out_specs=jax.tree.map(lambda _: pl.BlockSpec(memory_space=pltpu.VMEM), out_shape),
        scratch_shapes=list(scratch),
        compiler_params=pltpu.CompilerParams(vmem_limit_bytes=VMEM_BYTES),
    )


def sds(shape, dtype):
    return jax.ShapeDtypeStruct(shape, dtype)


def nn(a, b):
    return lax.dot_general(a, b, (((1,), (0,)), ((), ())), preferred_element_type=F32)


def nt(a, b):
    return lax.dot_general(a, b, (((1,), (1,)), ((), ())), preferred_element_type=F32)


def tn(a, b):
    return lax.dot_general(a, b, (((0,), (0,)), ((), ())), preferred_element_type=F32)


def normalize(hidden):
    centre = hidden - jnp.mean(hidden, axis=-1, keepdims=True)
    inverse = lax.rsqrt(jnp.mean(centre * centre, axis=-1, keepdims=True) + NORM_EPSILON)
    return centre * inverse, inverse


def norm_backward(grad_normed, normal_rows, inverse, gain_row):
    scaled = grad_normed * gain_row
    return inverse * (
        scaled
        - jnp.mean(scaled, axis=-1, keepdims=True)
        - normal_rows * jnp.mean(scaled * normal_rows, axis=-1, keepdims=True)
    )


def head_masks():
    lane = lax.broadcasted_iota(jnp.int32, (1, LANES), 1) // HEAD_DIM
    return [lane == h for h in range(4)]


def stack_heads(rows, masks):
    zero = jnp.zeros_like(rows)
    return jnp.concatenate([jnp.where(mask, rows, zero) for mask in masks], axis=0)


def fold_heads(tall, masks):
    out = jnp.where(masks[0], tall[0:WROWS], 0.0)
    for h in range(1, 4):
        out = jnp.where(masks[h], tall[h * WROWS : (h + 1) * WROWS], out)
    return out


def attn_fwd_body(hid, vec, w_in, w_out, perm, perm_t, bias, mask, h_one, wn, qkv, mixed, attn):
    normal, _ = normalize(hid[...].astype(F32))
    normed = (normal * vec[0:1] + vec[1:2]).astype(BF)
    wn[...] = nn(perm[...], normed).astype(BF)
    in_bias = jnp.concatenate([vec[4:5], jnp.zeros((1, D), F32), vec[5:6]], axis=1)

    @pl.loop(0, 4)
    def _(t):
        rows = pl.ds(pl.multiple_of(t * 256, 256), 256)
        qkv[rows, :] = (nn(wn[rows, :], w_in[...]) + in_bias).astype(BF)

    masks = head_masks()

    @pl.loop(0, WINDOWS)
    def _(w):
        rows = pl.ds(pl.multiple_of(w * WROWS, WROWS), WROWS)
        allow = mask[w] > 0.0
        allow = jnp.concatenate([allow, allow], axis=1)
        for g in range(QUADS):
            cols = slice(g * LANES, (g + 1) * LANES)
            q4 = stack_heads(qkv[rows, g * LANES : (g + 1) * LANES], masks)
            kg = qkv[rows, D + g * LANES : D + (g + 1) * LANES]
            vg = qkv[rows, 2 * D + g * LANES : 2 * D + (g + 1) * LANES]
            s = jnp.where(allow, nt(kg, q4) * SCALE + bias[g], -1e30)
            e = jnp.exp(s - jnp.max(s, axis=0, keepdims=True))
            a = e * (1.0 / jnp.sum(e, axis=0, keepdims=True))
            attn[w * QUADS + g] = a
            mixed[rows, cols] = fold_heads(tn(a.astype(BF), vg), masks).astype(BF)

    back = nn(perm_t[...], mixed[...]).astype(BF)
    h_one[...] = hid[...].astype(F32) + nn(back, w_out[...]) + vec[6:7]


def attn_fwd(hid, vec, w_in, w_out, perm, perm_t, bias, mask):
    return call(
        attn_fwd_body,
        (
            sds((CELLS, D), F32),
            sds((WTOK, D), BF),
            sds((WTOK, 3 * D), BF),
            sds((WTOK, D), BF),
            sds((WINDOWS * QUADS, WROWS, PAIR), F32),
        ),
        8,
    )(hid, vec, w_in, w_out, perm, perm_t, bias, mask)


def moe_fwd_body(
    h_one, vec, w1, w2, b1, router, router_bias, chosen, onehot, onehot_t,
    out, normed_two, disp, act, slope, picked, gate, other, rows_out,
):
    normal, _ = normalize(h_one[...])
    two = (normal * vec[2:3] + vec[3:4]).astype(BF)
    normed_two[...] = two
    logits = nn(two, router[...])
    gap = (logits[:, LANES:] + router_bias[1:2]) - (logits[:, :LANES] + router_bias[0:1])
    gap = jnp.where(chosen[...] > 0.0, gap, -gap)
    gate[...] = 1.0 / (1.0 + jnp.exp(-gap))
    other[...] = 1.0 / (1.0 + jnp.exp(gap))
    disp[...] = nn(onehot_t[...], two).astype(BF)

    @pl.loop(0, 4)
    def _(t):
        rows = pl.ds(pl.multiple_of(t * 256, 256), 256)
        e = t // 2
        own = disp[rows, :]
        for c in range(3):
            cols = slice(c * 512, (c + 1) * 512)
            pre = nn(own, w1[e, :, cols]) + b1[pl.ds(e, 1), cols]
            phi = 0.5 * (1.0 + lax.erf(pre * 0.7071067811865476))
            act[rows, cols] = (pre * phi).astype(BF)
            slope[rows, cols] = (
                phi + pre * jnp.exp(-0.5 * pre * pre) * 0.3989422804014327
            ).astype(BF)
        rows_out[rows, :] = (nn(act[rows, :], w2[e]) + vec[pl.ds(7 + e, 1)]).astype(BF)

    taken = nn(onehot[...], rows_out[...])
    picked[...] = taken.astype(BF)
    for c in range(3):
        cols = slice(c * LANES, (c + 1) * LANES)
        out[:, cols] = (h_one[:, cols] + gate[...] * taken[:, cols]).astype(out.dtype)


def moe_fwd(h_one, vec, w1, w2, b1, router, router_bias, chosen, onehot, onehot_t, out_dtype):
    return call(
        moe_fwd_body,
        (
            sds((CELLS, D), out_dtype),
            sds((CELLS, D), BF),
            sds((SLOTS, D), BF),
            sds((SLOTS, F), BF),
            sds((SLOTS, F), BF),
            sds((CELLS, D), BF),
            sds((CELLS, LANES), F32),
            sds((CELLS, LANES), F32),
        ),
        10,
        scratch=[pltpu.VMEM((SLOTS, D), BF)],
    )(h_one, vec, w1, w2, b1, router, router_bias, chosen, onehot, onehot_t)


def moe_bwd_body(
    grad, h_one, vec, w1, w2, router_gap, chosen, onehot, onehot_t,
    normed_two, disp, act, slope, picked, gate, other,
    grad_one, dw1, dw2, db1, drouter, small, g_rows, g_pre, g_disp,
):
    go = grad[...].astype(F32)
    gate_wide = jnp.concatenate([gate[...]] * 3, axis=1)
    g_picked = (go * gate_wide).astype(BF)
    g_gate = jnp.sum(go * picked[...].astype(F32), axis=-1, keepdims=True)
    sign = jnp.where(chosen[...] > 0.0, 1.0, -1.0)
    gl = (g_gate * gate[...] * other[...] * sign).astype(BF).astype(F32)
    g_rows[...] = nn(onehot_t[...], g_picked).astype(BF)

    @pl.loop(0, EXPERTS)
    def _(e):
        total = jnp.zeros((1, F), F32)
        for t in range(2):
            rows = pl.ds(pl.multiple_of(e * 512 + t * 256, 256), 256)
            own = g_rows[rows, :]
            parts = []
            for c in range(3):
                cols = slice(c * 512, (c + 1) * 512)
                gp = (nt(own, w2[e, cols, :]) * slope[rows, cols].astype(F32)).astype(BF)
                g_pre[t * 256 : (t + 1) * 256, cols] = gp
                parts.append(jnp.sum(gp.astype(F32), axis=0, keepdims=True))
            total = total + jnp.concatenate(parts, axis=1)
            g_disp[rows, :] = nt(g_pre[t * 256 : (t + 1) * 256, :], w1[e]).astype(BF)
        db1[pl.ds(e, 1), :] = total
        both = pl.ds(pl.multiple_of(e * 512, 512), 512)
        small[pl.ds(7 + e, 1), :] = jnp.sum(g_rows[both, :].astype(F32), axis=0, keepdims=True)
        for c in range(3):
            cols = slice(c * 512, (c + 1) * 512)
            dw1[e, :, cols] = tn(disp[both, :], g_pre[:, cols])
            dw2[e, cols, :] = tn(act[both, cols], g_rows[both, :])

    g_two = nn(onehot[...], g_disp[...])
    gl_wide = jnp.concatenate([gl] * 3, axis=1)
    g_two = g_two + gl_wide * router_gap[0:1]
    lane = lax.broadcasted_iota(jnp.int32, (1, LANES), 1)
    drouter[...] = tn(normed_two[...], jnp.where(lane == 0, -gl, gl).astype(BF))
    normal, inverse = normalize(h_one[...])
    small[0:1] = jnp.zeros((1, D), F32)
    small[1:2] = jnp.zeros((1, D), F32)
    small[2:3] = jnp.sum(g_two * normal, axis=0, keepdims=True)
    small[3:4] = jnp.sum(g_two, axis=0, keepdims=True)
    small[4:7] = jnp.zeros((3, D), F32)
    small[9:16] = jnp.zeros((7, D), F32)
    small[9:10] = jnp.sum(gl_wide, axis=0, keepdims=True)
    grad_one[...] = go + norm_backward(g_two, normal, inverse, vec[2:3])


def moe_bwd(grad, h_one, vec, w1, w2, router_gap, chosen, onehot, onehot_t, saved):
    return call(
        moe_bwd_body,
        (
            sds((CELLS, D), F32),
            sds((EXPERTS, D, F), F32),
            sds((EXPERTS, F, D), F32),
            sds((8, F), F32),
            sds((D, LANES), F32),
            sds((16, D), F32),
        ),
        16,
        scratch=[pltpu.VMEM((SLOTS, D), BF), pltpu.VMEM((512, F), BF), pltpu.VMEM((SLOTS, D), BF)],
    )(grad, h_one, vec, w1, w2, router_gap, chosen, onehot, onehot_t, *saved)


def attn_bwd_body(
    grad_one, hid, vec, w_in, w_out, perm, perm_t, wn, qkv, mixed, attn,
    grad_in, dw_in, dw_out, dbias, small, g_mix, g_qkv,
):
    gao = grad_one[...].astype(BF)
    small[...] = jnp.zeros((16, D), F32)
    small[6:7] = jnp.sum(gao.astype(F32), axis=0, keepdims=True)
    gao_w = nn(perm[...], gao).astype(BF)
    dw_out[...] = tn(mixed[...], gao_w)
    g_mix[...] = nt(gao_w, w_out[...]).astype(BF)
    dbias[...] = jnp.zeros_like(dbias)
    masks = head_masks()

    @pl.loop(0, WINDOWS)
    def _(w):
        rows = pl.ds(pl.multiple_of(w * WROWS, WROWS), WROWS)
        for g in range(QUADS):
            cols = slice(g * LANES, (g + 1) * LANES)
            kcols = slice(D + g * LANES, D + (g + 1) * LANES)
            vcols = slice(2 * D + g * LANES, 2 * D + (g + 1) * LANES)
            q4 = stack_heads(qkv[rows, cols], masks)
            kg = qkv[rows, kcols]
            vg = qkv[rows, vcols]
            d4 = stack_heads(g_mix[rows, cols], masks)
            a = attn[w * QUADS + g]
            t = a * nt(vg, d4)
            ds = (t - a * jnp.sum(t, axis=0, keepdims=True)).astype(BF)
            dbias[g] += ds.astype(F32)
            g_qkv[rows, cols] = (fold_heads(tn(ds, kg), masks) * SCALE).astype(BF)
            g_qkv[rows, kcols] = (nn(ds, q4) * SCALE).astype(BF)
            g_qkv[rows, vcols] = nn(a.astype(BF), d4).astype(BF)

    small[4:5] = jnp.sum(g_qkv[:, :D].astype(F32), axis=0, keepdims=True)
    small[5:6] = jnp.sum(g_qkv[:, 2 * D :].astype(F32), axis=0, keepdims=True)
    for c in range(3):
        cols = slice(c * D, (c + 1) * D)
        dw_in[:, cols] = tn(wn[...], g_qkv[:, cols])
    g_flat = nn(perm_t[...], g_qkv[...]).astype(BF)
    g_normed = nt(g_flat, w_in[...])
    normal, inverse = normalize(hid[...].astype(F32))
    small[0:1] = jnp.sum(g_normed * normal, axis=0, keepdims=True)
    small[1:2] = jnp.sum(g_normed, axis=0, keepdims=True)
    grad_in[...] = grad_one[...] + norm_backward(g_normed, normal, inverse, vec[0:1])


def attn_bwd(grad_one, hid, vec, w_in, w_out, perm, perm_t, saved):
    return call(
        attn_bwd_body,
        (
            sds((CELLS, D), F32),
            sds((D, 3 * D), F32),
            sds((D, D), F32),
            sds((QUADS, WROWS, PAIR), F32),
            sds((16, D), F32),
        ),
        11,
        scratch=[pltpu.VMEM((WTOK, D), BF), pltpu.VMEM((WTOK, 3 * D), BF)],
    )(grad_one, hid, vec, w_in, w_out, perm, perm_t, *saved)


def window_source(shifted):
    source = np.full((WTOK,), -1, np.int32)
    for w in range(WINDOWS):
        for p in range(WIN * WIN):
            r, s = (w // 4) * WIN + p // WIN, (w % 4) * WIN + p % WIN
            if shifted:
                r, s = (r + SHIFT) % SIDE, (s + SHIFT) % SIDE
            source[w * WROWS + p] = r * SIDE + s
    return source


def window_perm(shifted):
    source = window_source(shifted)
    return (source[:, None] == np.arange(CELLS)[None, :]).astype(np.float32)


def wrap_codes(shifted):
    code = np.zeros((CELLS,), np.float32)
    if shifted:
        for r in range(SIDE):
            for s in range(SIDE):
                rr, ss = (r - SHIFT) % SIDE, (s - SHIFT) % SIDE
                code[r * SIDE + s] = 2 * (rr >= SIDE - SHIFT) + (ss >= SIDE - SHIFT)
    return code


def relative_onehot():
    table = np.zeros((WROWS, WROWS, RELS), np.float32)
    for j in range(WIN * WIN):
        for i in range(WIN * WIN):
            a = i // WIN - j // WIN + WIN - 1
            b = i % WIN - j % WIN + WIN - 1
            table[j, i, a * (2 * WIN - 1) + b] = 1.0
    return table


def window_masks(items, shifted, perm_t):
    labels = items.astype(F32)
    if shifted:
        labels = labels * 4.0 + jnp.asarray(wrap_codes(True))
    placed = nn(jnp.broadcast_to((labels + 1.0).astype(BF), (8, CELLS)), perm_t)[0]
    placed = placed.reshape(WINDOWS, WROWS)
    same = (placed[:, :, None] == placed[:, None, :]) & (placed[:, :, None] > 0.0)
    same = same.astype(F32)
    return jnp.concatenate([same, same], axis=2)


def bias_tables(position_table):
    rel = jnp.asarray(relative_onehot().reshape(WROWS * WROWS, RELS), BF)
    rows = lax.dot_general(
        position_table.astype(BF), rel, (((0,), (1,)), ((), ())), preferred_element_type=F32
    )
    rows = rows.reshape(QUADS, 4, WROWS, WROWS)
    return jnp.transpose(rows, (0, 2, 1, 3)).reshape(QUADS, WROWS, PAIR)


def bias_table_grad(dbias):
    rel = jnp.asarray(relative_onehot().reshape(WROWS * WROWS, RELS), BF)
    rows = jnp.transpose(dbias.reshape(QUADS, WROWS, 4, WROWS), (0, 2, 1, 3))
    rows = rows.reshape(HEADS, WROWS * WROWS)
    high = rows.astype(BF)
    low = (rows - high.astype(F32)).astype(BF)
    both = nn(jnp.concatenate([high, low], axis=0), rel)
    return (both[:HEADS] + both[HEADS:]).T


def slot_tables(routes, slots):
    group = (jnp.arange(CELLS, dtype=jnp.int32) // GROUP) * CAP
    place = routes * (2 * CAP) + group + slots
    wide = jnp.arange(SLOTS, dtype=jnp.int32)
    onehot = (place[:, None] == wide[None, :]).astype(BF)
    onehot_t = (wide[:, None] == place[None, :]).astype(BF)
    chosen = jnp.broadcast_to(routes[:, None].astype(F32), (CELLS, LANES))
    return onehot, onehot_t, chosen

LEAD = 73
SMALL = 9326
LAG = LEAD * LANES - SMALL
SPANS = ((LEAD, D, 9), (LEAD + 3456, D, 3), (LEAD + 4608, 2 * D, 12), (LEAD + 4608 + 9216, 2 * F, 3))
ALIGNED = LEAD + 4608 + 2 * 9216


def unpack_body(rows, devices, padded, got, w_in, w_out, w1, w2, flat):
    @pl.loop(0, devices)
    def _(d):
        flat[pl.ds(d * rows, rows), :] = got[pl.ds(pl.multiple_of(d * padded, 16), rows), :].astype(F32)

    lane = lax.broadcasted_iota(jnp.int32, (1, LANES), 1)
    for (base, height, tiles), out in zip(SPANS, (w_in, w_out, w1, w2)):
        step = 64

        @pl.loop(0, height // step)
        def _(t, base=base, tiles=tiles, out=out):
            first = base - 1 + t * (step * tiles)
            before = flat[pl.ds(first, step, stride=tiles), :]
            for j in range(tiles):
                here = flat[pl.ds(first + 1 + j, step, stride=tiles), :]
                tile = pltpu.roll(jnp.where(lane >= LANES - LAG, before, here), LAG, 1)
                out[pl.ds(pl.multiple_of(t * step, step), step), j * LANES : (j + 1) * LANES] = tile.astype(BF)
                before = here


def unpack_weights(gathered, rows, devices):
    padded = gathered.shape[0] // devices
    return call(
        functools.partial(unpack_body, rows, devices, padded),
        (sds((D, 3 * D), BF), sds((D, D), BF), sds((2 * D, F), BF), sds((2 * F, D), BF)),
        1,
        scratch=[pltpu.VMEM((devices * rows + 8, LANES), F32)],
    )(gathered)


def pack_body(rows, devices, padded, orders, small, dw_in, dw_out, dw1, dw2, part_a, part_b, al):
    al[0:LEAD, :] = small[0:LEAD, :]
    tail = al.shape[0] - ALIGNED
    al[pl.ds(ALIGNED, tail), :] = jnp.zeros((tail, LANES), F32)
    for (base, height, tiles), grad in zip(SPANS, (dw_in, dw_out, dw1, dw2)):
        step = 64

        @pl.loop(0, height // step)
        def _(t, base=base, tiles=tiles, grad=grad):
            first = base + t * (step * tiles)
            own = pl.ds(pl.multiple_of(t * step, step), step)
            for j in range(tiles):
                al[pl.ds(first + j, step, stride=tiles), :] = grad[own, j * LANES : (j + 1) * LANES]

    half = padded // 2
    for at, (order, part) in enumerate(zip(orders, (part_a, part_b))):
        count = len(order)

        @pl.loop(0, devices)
        def _(k, at=at, order=order, part=part):
            device = 0
            for place, bit in enumerate(order):
                device = device + (((k >> (count - 1 - place)) & 1) << bit)
            part[k] = al[pl.ds(device * rows + at * half, half), :].astype(BF)


def pack_grads(small, dw_in, dw_out, dw1, dw2, rows, devices, padded, orders):
    half = padded // 2
    return call(
        functools.partial(pack_body, rows, devices, padded, orders),
        (sds((devices, half, LANES), BF), sds((devices, half, LANES), BF)),
        5,
        scratch=[pltpu.VMEM((devices * rows + padded, LANES), F32)],
    )(small, dw_in, dw_out, dw1, dw2)


def flip_pairs(axis, bit):
    return [(i, i ^ (1 << bit)) for i in range(lax.axis_size(axis))]


def stage_orders():
    dp, fsdp = (lax.axis_size(axis).bit_length() - 1 for axis in (DP, FSDP))
    rest = [(DP, bit) for bit in range(1, dp)] + [(FSDP, bit) for bit in range(2, fsdp)]
    core, x, y = (FSDP, 0), (FSDP, 1), (DP, 0)
    return [core, y, x] + rest, [core, x, y] + rest


def device_bit(axis, bit):
    return bit if axis == FSDP else bit + lax.axis_size(FSDP).bit_length() - 1


def halve(keep, axis, bit):
    half = keep.shape[0] // 2
    mine = (lax.axis_index(axis) >> bit) & 1
    send = lax.dynamic_slice_in_dim(keep, (1 - mine) * half, half).astype(BF)
    got = lax.ppermute(send, axis, flip_pairs(axis, bit))
    return lax.dynamic_slice_in_dim(keep, mine * half, half).astype(F32) + got.astype(F32)


def shards(inputs, items, routes, slots, cotangent, params, momentum, average):
    fsdp, dp = lax.axis_size(FSDP), lax.axis_size(DP)
    devices = fsdp * dp
    share = params.shape[1]
    rows = share // LANES
    padded = -(-(rows + 1) // 32) * 32
    step_rate = RATE_BASE / math.sqrt(CELLS * devices)
    orders = stage_orders()
    places = [[device_bit(*stage) for stage in order] for order in orders]

    pieces, perms, tables = [], [], []
    hidden = inputs.reshape(CELLS, D)
    gathered = []
    for b in range(BLOCKS):
        own = params[b].astype(BF).reshape(rows, LANES)
        own = jnp.pad(own, ((0, padded - rows), (0, 0)))
        gathered.append(lax.all_gather(own, (DP, FSDP), axis=0, tiled=True))
    saves = []
    for b in range(BLOCKS):
        shifted = b % 2 == 1
        one = window_perm(shifted)
        perm, perm_t = jnp.asarray(one, BF), jnp.asarray(one.T, BF)
        mask = window_masks(items.reshape(CELLS), shifted, perm_t)
        table = slot_tables(routes[b].reshape(CELLS), slots[b].reshape(CELLS))
        w_in, w_out, w1, w2 = unpack_weights(gathered[b], rows, devices)
        w1, w2 = w1.reshape(EXPERTS, D, F), w2.reshape(EXPERTS, F, D)
        flat = gathered[b][:LEAD].astype(F32).reshape(-1)
        small = unpack_small(flat)
        bias = bias_tables(small.position_table)
        vec = jnp.concatenate([small.norms, small.biases, small.expert_out_bias, jnp.zeros((7, D), F32)])
        b1 = jnp.pad(small.expert_in_bias, ((0, 6), (0, 0)))
        rw = small.router_weight
        router = jnp.concatenate([jnp.broadcast_to(rw[:, e : e + 1], (D, LANES)) for e in range(2)], axis=1).astype(BF)
        gap = jnp.broadcast_to((rw[:, 1] - rw[:, 0])[None], (8, D))
        rb = jnp.broadcast_to(small.router_bias[:, None], (2, LANES))
        h_one, *kept_attn = attn_fwd(hidden, vec, w_in, w_out, perm, perm_t, bias, mask)
        last = b == BLOCKS - 1
        following, *kept_moe = moe_fwd(h_one, vec, w1, w2, b1, router, rb, table[2], table[0], table[1], BF if last else F32)
        saves.append((hidden, h_one, vec, w_in, w_out, w1, w2, gap, perm, perm_t, table, kept_attn, kept_moe))
        hidden = following
    outputs = hidden.reshape(1, CELLS, D)

    gradient = cotangent.reshape(CELLS, D)
    sums = [None] * BLOCKS
    vectors = [None] * BLOCKS
    for b in range(BLOCKS - 1, -1, -1):
        hidden, h_one, vec, w_in, w_out, w1, w2, gap, perm, perm_t, table, kept_attn, kept_moe = saves[b]
        g_one, dw1, dw2, db1, drouter, small_moe = moe_bwd(
            gradient, h_one, vec, w1, w2, gap, table[2], table[0], table[1], kept_moe
        )
        gradient, dw_in, dw_out, dbias, small_attn = attn_bwd(g_one, hidden, vec, w_in, w_out, perm, perm_t, kept_attn)
        both = small_moe + small_attn
        flat = jnp.concatenate(
            [
                jnp.zeros((LAG,), F32),
                both[0:4].reshape(-1),
                bias_table_grad(dbias).reshape(-1),
                both[4:7].reshape(-1),
                drouter[:, :2].reshape(-1),
                jnp.stack([-both[9, 0], both[9, 0]]),
                db1[:2].reshape(-1),
                both[7:9].reshape(-1),
            ]
        )
        small = flat.reshape(LEAD, LANES)
        vectors[b] = both[0:9]
        parts = pack_grads(
            small, dw_in, dw_out, dw1.reshape(2 * D, F), dw2.reshape(2 * F, D), rows, devices, padded, places
        )
        done = []
        for part, order in zip(parts, orders):
            for stage in order:
                part = halve(part, *stage)
            done.append(part[0])
        total = jnp.concatenate(done, axis=0).reshape(-1)
        sums[b] = total[LAG : LAG + share]
    vector_grads = jnp.stack(vectors)
    for axis, bit in orders[0]:
        vector_grads = vector_grads + lax.ppermute(vector_grads, axis, flip_pairs(axis, bit))
    grad_all = jnp.stack(sums)
    new_momentum = MOMENTUM_DECAY * momentum + grad_all
    new_params = params - step_rate * (grad_all + MOMENTUM_DECAY * new_momentum)
    new_average = AVERAGE_DECAY * average + (1.0 - AVERAGE_DECAY) * new_params
    return outputs, gradient.reshape(1, CELLS, D), new_params, new_momentum, new_average, vector_grads


class Small(NamedTuple):
    norms: Any
    position_table: Any
    biases: Any
    router_weight: Any
    router_bias: Any
    expert_in_bias: Any
    expert_out_bias: Any


def unpack_small(flat):
    shapes = ((4, D), (RELS, HEADS), (3, D), (D, EXPERTS), (EXPERTS,), (EXPERTS, F), (EXPERTS, D))
    cuts = [0]
    for shape in shapes:
        cuts.append(cuts[-1] + math.prod(shape))
    return Small(*[flat[a:b].reshape(shape) for a, b, shape in zip(cuts, cuts[1:], shapes)])


def solution(mesh):
    both = (DP, FSDP)
    canvas, vector = P(both), P(None, both)
    return jax.shard_map(
        shards,
        mesh=mesh,
        in_specs=(canvas, canvas, vector, vector, canvas, vector, vector, vector),
        out_specs=(canvas, canvas, vector, vector, vector, P()),
        check_vma=False,
    )
```

profile of v0, /device:TPU:0, one launch (start us, length us, event | category | flops | bytes accessed | tf_op | source)
XLA Modules:
  0.0 506.8 jit_solution(12826367972461822107)
XLA Ops:
  20.9 2.0 fusion.onehot_t
  22.9 59.4 %all-gather.5.cloned.1.call-done.got = bf16[23552,128]{1,0:T(8,128)(2,1)} async-done(((bf16[736,128]{1,0:T(8,128)(2,1)}), bf16[23552,128]{1,0:T(8,128)(2,1)}) %all-gather.5.cloned.1.call-update) | async-done | bytes 6029328 | tf_op jit(solution)/shard_map/all_gather | solution.py:521
  83.4 69.5 %all-gather.3.cloned.1.call-done.got = bf16[23552,128]{1,0:T(8,128)(2,1)} async-done(((bf16[736,128]{1,0:T(8,128)(2,1)}), bf16[23552,128]{1,0:T(8,128)(2,1)}) %all-gather.3.cloned.1.call-update) | async-done | bytes 6029328 | tf_op jit(solution)/shard_map/all_gather | solution.py:521
  153.9 3.9 slice.170
  160.4 3.9 slice.184
  175.0 12.9 %shard_map.208 = (bf16[384,1152]{1,0:T(8,128)(2,1)}, bf16[384,384]{1,0:T(8,128)(2,1)}, bf16[768,1536]{1,0:T(8,128)(2,1)}, bf16[3072,384]{1,0:T(8,128)(2,1)}) custom-call(bf16[23552,128]{1,0:T(8,128)(2,1)} %all-gather.3.cloned.1.call-done.got), custom_call_target="tpu_custom_call" | custom-call | tf_op jit(solution)/shard_map/pallas_call | solution.py:438
  188.0 19.8 %shard_map.209 = (f32[784,384]{1,0:T(8,128)}, bf16[1024,384]{1,0:T(8,128)(2,1)}, bf16[1024,1152]{1,0:T(8,128)(2,1)}, bf16[1024,384]{1,0:T(8,128)(2,1)}, f32[48,64,256]{2,1,0:T(8,128)}) custom-call(bf16[784,384]{1,0:T(8,128)(2,1)} %bitcast.89, f32[16,384]{1,0:T(8,128)} %get-tuple-element.164.vec, bf16[384,1152]{1,0:T(8,128)(2,1)} %get-tuple-element.66.w_in, ...), custom_call_target="tpu_custom_call" | custom-call | tf_op jit(solution)/shard_map/pallas_call | solution.py:140
  209.3 14.9 %shard_map.210 = (f32[784,384]{1,0:T(8,128)}, bf16[784,384]{1,0:T(8,128)(2,1)}, bf16[1024,384]{1,0:T(8,128)(2,1)}, bf16[1024,1536]{1,0:T(8,128)(2,1)}, bf16[1024...) custom-call(f32[784,384]{1,0:T(8,128)} %get-tuple-element.68.h_one, ...), custom_call_target="tpu_custom_call" | custom-call | tf_op jit(solution)/shard_map/pallas_call | solution.py:190
  224.2 12.7 %shard_map.211 = (bf16[384,1152]{1,0:T(8,128)(2,1)}, bf16[384,384]{1,0:T(8,128)(2,1)}, bf16[768,1536]{1,0:T(8,128)(2,1)}, bf16[3072,384]{1,0:T(8,128)(2,1)}) custom-call(bf16[23552,128]{1,0:T(8,128)(2,1)} %all-gather.5.cloned.1.call-done.got), custom_call_target="tpu_custom_call" | custom-call | tf_op jit(solution)/shard_map/pallas_call | solution.py:438
  237.0 19.9 %shard_map.212 = (f32[784,384]{1,0:T(8,128)}, bf16[1024,384]{1,0:T(8,128)(2,1)}, bf16[1024,1152]{1,0:T(8,128)(2,1)}, bf16[1024,384]{1,0:T(8,128)(2,1)}, f32[48,64,256]{2,1,0:T(8,128)}) custom-call(f32[784,384]{1,0:T(8,128)} %get-tuple-element.71.hid, f32[16,384]{1,0:T(8,128)} %get-tuple-element.163.vec, bf16[384,1152]{1,0:T(8,128)(2,1)} %get-tuple-element.72.w_in, ...), custom_call_target="tpu_custom_call" | custom-call | tf_op jit(solution)/shard_map/pallas_call | solution.py:140
  258.4 14.9 %shard_map.213 = (bf16[784,384]{1,0:T(8,128)(2,1)}, bf16[784,384]{1,0:T(8,128)(2,1)}, bf16[1024,384]{1,0:T(8,128)(2,1)}, bf16[1024,1536]{1,0:T(8,128)(2,1)}, bf1...) custom-call(f32[784,384]{1,0:T(8,128)} %get-tuple-element.74.h_one, ...), custom_call_target="tpu_custom_call" | custom-call | tf_op jit(solution)/shard_map/pallas_call | solution.py:190
  273.9 18.2 %shard_map.214 = (f32[784,384]{1,0:T(8,128)}, f32[2,384,1536]{2,1,0:T(8,128)}, f32[2,1536,384]{2,1,0:T(8,128)}, f32[8,1536]{1,0:T(8,128)}, f32[384,128]{1,0:T(8,128)}, /*index=5*/f32[16,384]{1,0:T(8,128)}) custom-call(bf16[784,384]{1,0:T(8,128)(2,1)} %bitcast.95, f32[784,384]{1,0:T(8,128)} %get-tuple-element.74.h_one, f32[16,384]{1,0:T(8,128)} %get-tuple-element.163.vec, ...), custom_call_target="tpu_custom_call" | custom-call | tf_op jit(solution)/shard_map/pallas_call | solution.py:259
  292.1 26.8 %shard_map.215 = (f32[784,384]{1,0:T(8,128)}, f32[384,1152]{1,0:T(8,128)}, f32[384,384]{1,0:T(8,128)}, f32[3,64,256]{2,1,0:T(8,128)}, f32[16,384]{1,0:T(8,128)}) custom-call(f32[784,384]{1,0:T(8,128)} %get-tuple-element.85.grad_one, f32[784,384]{1,0:T(8,128)} %get-tuple-element.71.hid, f32[16,384]{1,0:T(8,128)} %get-tuple-element.163.vec, ...), custom_call_target="tpu_custom_call" | custom-call | tf_op jit(solution)/shard_map/pallas_call | solution.py:320
  319.5 18.3 %shard_map.216 = (f32[784,384]{1,0:T(8,128)}, f32[2,384,1536]{2,1,0:T(8,128)}, f32[2,1536,384]{2,1,0:T(8,128)}, f32[8,1536]{1,0:T(8,128)}, f32[384,128]{1,0:T(8,128)}, /*index=5*/f32[16,384]{1,0:T(8,128)}) custom-call(f32[784,384]{1,0:T(8,128)} %get-tuple-element.90.grad, f32[784,384]{1,0:T(8,128)} %get-tuple-element.68.h_one, ...), custom_call_target="tpu_custom_call" | custom-call | tf_op jit(solution)/shard_map/pallas_call | solution.py:259
  337.9 26.7 %shard_map.217 = (f32[784,384]{1,0:T(8,128)}, f32[384,1152]{1,0:T(8,128)}, f32[384,384]{1,0:T(8,128)}, f32[3,64,256]{2,1,0:T(8,128)}, f32[16,384]{1,0:T(8,128)}) custom-call(f32[784,384]{1,0:T(8,128)} %get-tuple-element.98.grad_one, bf16[784,384]{1,0:T(8,128)(2,1)} %bitcast.90, f32[16,384]{1,0:T(8,128)} %get-tuple-element.164.vec, ...), custom_call_target="tpu_custom_call" | custom-call | tf_op jit(solution)/shard_map/pallas_call | solution.py:320
  371.9 9.3 %shard_map.218 = (bf16[32,368,128]{2,1,0:T(8,128)(2,1)}, bf16[32,368,128]{2,1,0:T(8,128)(2,1)}) custom-call(f32[73,128]{1,0:T(8,128)} %bitcast.101, f32[384,1152]{1,0:T(8,128)} %get-tuple-element.109.dw_in, f32[384,384]{1,0:T(8,128)} %get-tuple-element.110.dw_out, f32[768,1536]{1,0:T(8,128)} %bitcast.87, f32[3072,384]{1,0:T(8,128)} %bitcast.88), custom_call_target="tpu_custom_call" | custom-call | tf_op jit(solution)/shard_map/pallas_call | solution.py:474
  381.2 2.7 constant_dynamic-slice_fusion.2
  386.4 2.6 constant_dynamic-slice_fusion.3
  391.2 9.6 %shard_map.219 = (bf16[32,368,128]{2,1,0:T(8,128)(2,1)}, bf16[32,368,128]{2,1,0:T(8,128)(2,1)}) custom-call(f32[73,128]{1,0:T(8,128)} %bitcast.100, f32[384,1152]{1,0:T(8,128)} %get-tuple-element.120.dw_in, f32[384,384]{1,0:T(8,128)} %get-tuple-element.121.dw_out, f32[768,1536]{1,0:T(8,128)} %bitcast.85, f32[3072,384]{1,0:T(8,128)} %bitcast.86), custom_call_target="tpu_custom_call" | custom-call | tf_op jit(solution)/shard_map/pallas_call | solution.py:474
  400.9 2.8 constant_dynamic-slice_fusion
  409.6 2.7 collective-permute-done.22
  412.3 2.1 collective-permute-start.23
  414.3 2.1 collective-permute-done.23
  416.4 2.4 collective-permute-start.24
  418.8 2.7 collective-permute-done.24
  434.2 9.7 %collective-permute-done.6 = bf16[8,368,128]{2,1,0:T(8,128)(2,1)S(1)} collective-permute-done((bf16[8,368,128]{2,1,0:T(8,128)(2,1)S(1)}, bf16[8,368,128]{2,1,0:T(8,128)(2,1)S(1)}, u32[]{:S(2)}, u32[]{:S(2)}) %collective-permute-start.6) | collective-permute-done | bytes 753696 | tf_op jit(solution)/shard_map/ppermute | solution.py:501
  448.2 11.8 %collective-permute-done.16 = bf16[8,368,128]{2,1,0:T(8,128)(2,1)S(1)} collective-permute-done((bf16[8,368,128]{2,1,0:T(8,128)(2,1)S(1)}, bf16[8,368,128]{2,1,0:T(8,128)(2,1)S(1)}, u32[]{:S(2)}, u32[]{:S(2)}) %collective-permute-start.16) | collective-permute-done | bytes 753696 | tf_op jit(solution)/shard_map/ppermute | solution.py:501
  464.4 5.9 %collective-permute-done.7 = bf16[4,368,128]{2,1,0:T(8,128)(2,1)S(1)} collective-permute-done((bf16[4,368,128]{2,1,0:T(8,128)(2,1)S(1)}, bf16[4,368,128]{2,1,0:T(8,128)(2,1)S(1)}, u32[]{:S(2)}, u32[]{:S(2)}) %collective-permute-start.7) | collective-permute-done | bytes 376864 | tf_op jit(solution)/shard_map/ppermute | solution.py:501
  476.7 4.2 collective-permute-done.8
  485.5 2.8 collective-permute-start.19
  490.4 3.2 collective-permute-done.19
  496.2 3.3 multiply_add_fusion
  (257 shorter events, 86.5 us)
Async XLA Ops:
  7.2 75.2 %all-gather.5.cloned.1.call-start = ((), (), s32[]{:S(2)}) async-start(), calls=%async_computation.1 | async-start | bytes 6217728 | tf_op jit(solution)/shard_map/all_gather | solution.py:521
  11.4 141.5 %all-gather.3.cloned.1.call-start = ((), (), s32[]{:S(2)}) async-start(), calls=%async_computation | async-start | bytes 6217728 | tf_op jit(solution)/shard_map/all_gather | solution.py:521
  337.8 26.8 %copy-start.18 = (f32[16,384]{1,0:T(8,128)S(1)}, f32[16,384]{1,0:T(8,128)}, u32[]{:S(2)}) copy-start(f32[16,384]{1,0:T(8,128)} %get-tuple-element.104) | copy-start | bytes 73732
  337.8 28.9 %copy-start.13 = (f32[384,128]{1,0:T(8,128)S(1)}, f32[384,128]{1,0:T(8,128)}, u32[]{:S(2)}) copy-start(f32[384,128]{1,0:T(8,128)} %get-tuple-element.107) | copy-start | bytes 589828
  337.9 29.0 %copy-start.16 = (f32[16,384]{1,0:T(8,128)S(1)}, f32[16,384]{1,0:T(8,128)}, u32[]{:S(2)}) copy-start(f32[16,384]{1,0:T(8,128)} %get-tuple-element.115) | copy-start | bytes 73732
  337.9 29.0 %copy-start.17 = (f32[16,384]{1,0:T(8,128)S(1)}, f32[16,384]{1,0:T(8,128)}, u32[]{:S(2)}) copy-start(f32[16,384]{1,0:T(8,128)} %get-tuple-element.116) | copy-start | bytes 73732
  367.8 36.1 %collective-permute-start.20 = (f32[2,9,384]{2,1,0:T(8,128)S(1)}, f32[2,9,384]{2,1,0:T(8,128)S(1)}, u32[]{:S(2)}, u32[]{:S(2)}) collective-permute-start(f32[2,9,384]{2,1,0:T(8,128)S(1)} %pad_maximum_fusion.7), channel_id=1, source_target_pairs={{0,1},{1,0},{2,3},{3,2},{4,5},{5,4},{6,7},{7,6},{8,9},{9,8},{10,11... | collective-permute-start | bytes 82952 | tf_op jit(solution)/shard_map/ppermute | solution.py:583
  383.9 38.2 %collective-permute-start.5 = (bf16[16,368,128]{2,1,0:T(8,128)(2,1)}, bf16[16,368,128]{2,1,0:T(8,128)(2,1)}, u32[]{:S(2)}, u32[]{:S(2)}) collective-permute-start(bf16[16,368,128]{2,1,0:T(8,128)(2,1)} %constant_dynamic-slice_fusion.2), channel_id=1, source_target_pairs={{0,1},{1,0},{2,3},{3,2},{4,5},{5,4},{6,7},{7,6},{8,9},{9,8},{10,11... | collective-permute-start | bytes 4521992 | tf_op jit(solution)/shard_map/ppermute | solution.py:501
  389.0 36.5 %collective-permute-start = (bf16[16,368,128]{2,1,0:T(8,128)(2,1)}, bf16[16,368,128]{2,1,0:T(8,128)(2,1)}, u32[]{:S(2)}, u32[]{:S(2)}) collective-permute-start(bf16[16,368,128]{2,1,0:T(8,128)(2,1)} %constant_dynamic-slice_fusion.3), channel_id=1, source_target_pairs={{0,1},{1,0},{2,3},{3,2},{4,5},{5,4},{6,7},{7,6},{8,9},{9,8},{10,11... | collective-permute-start | bytes 4521992 | tf_op jit(solution)/shard_map/ppermute | solution.py:501
  403.7 18.5 %copy-start.5 = (bf16[32,368,128]{2,1,0:T(8,128)(2,1)S(1)}, bf16[32,368,128]{2,1,0:T(8,128)(2,1)}, u32[]{:S(2)}) copy-start(bf16[32,368,128]{2,1,0:T(8,128)(2,1)} %get-tuple-element.114) | copy-start | bytes 9043972
  403.7 24.6 %collective-permute-start.15 = (bf16[16,368,128]{2,1,0:T(8,128)(2,1)}, bf16[16,368,128]{2,1,0:T(8,128)(2,1)}, u32[]{:S(2)}, u32[]{:S(2)}) collective-permute-start(bf16[16,368,128]{2,1,0:T(8,128)(2,1)} %constant_dynamic-slice_fusion), channel_id=1, source_target_pairs={{0,1},{1,0},{2,3},{3,2},{4,5},{5,4},{6,7},{7,6},{8,9},{9,8},{10,11... | collective-permute-start | bytes 4521992 | tf_op jit(solution)/shard_map/ppermute | solution.py:501
  403.9 4.2 collective-permute-start.21
  406.7 25.0 %collective-permute-start.10 = (bf16[16,368,128]{2,1,0:T(8,128)(2,1)}, bf16[16,368,128]{2,1,0:T(8,128)(2,1)}, u32[]{:S(2)}, u32[]{:S(2)}) collective-permute-start(bf16[16,368,128]{2,1,0:T(8,128)(2,1)} %constant_dynamic-slice_fusion.1), channel_id=1, source_target_pairs={{0,1},{1,0},{2,3},{3,2},{4,5},{5,4},{6,7},{7,6},{8,9},{9,8},{10,11... | collective-permute-start | bytes 4521992 | tf_op jit(solution)/shard_map/ppermute | solution.py:501
  408.1 4.2 collective-permute-start.22
  412.3 4.2 collective-permute-start.23
  416.4 5.0 collective-permute-start.24
  424.1 19.8 %collective-permute-start.6 = (bf16[8,368,128]{2,1,0:T(8,128)(2,1)S(1)}, bf16[8,368,128]{2,1,0:T(8,128)(2,1)S(1)}, u32[]{:S(2)}, u32[]{:S(2)}) collective-permute-start(bf16[8,368,128]{2,1,0:T(8,128)(2,1)S(1)} %dynamic-slice_convert_fusion.2), channel_id=1, source_target_pairs={{0,2},{1,3},{2,0},{3,1},{4,6},{5,7},{6,4},{7,5},{8,10},{9,11},{10,... | collective-permute-start | bytes 2261000 | tf_op jit(solution)/shard_map/ppermute | solution.py:501
  427.5 19.8 %collective-permute-start.1 = (bf16[8,368,128]{2,1,0:T(8,128)(2,1)S(1)}, bf16[8,368,128]{2,1,0:T(8,128)(2,1)S(1)}, u32[]{:S(2)}, u32[]{:S(2)}) collective-permute-start(bf16[8,368,128]{2,1,0:T(8,128)(2,1)S(1)} %dynamic-slice_convert_fusion.3), channel_id=1, source_target_pairs={{0,4},{4,0},{8,12},{12,8},{16,20},{20,16},{24,28},{28,24},{1,5},{5... | collective-permute-start | bytes 2261000 | tf_op jit(solution)/shard_map/ppermute | solution.py:501
  430.2 29.9 %collective-permute-start.16 = (bf16[8,368,128]{2,1,0:T(8,128)(2,1)S(1)}, bf16[8,368,128]{2,1,0:T(8,128)(2,1)S(1)}, u32[]{:S(2)}, u32[]{:S(2)}) collective-permute-start(bf16[8,368,128]{2,1,0:T(8,128)(2,1)S(1)} %dynamic-slice_convert_fusion), channel_id=1, source_target_pairs={{0,2},{1,3},{2,0},{3,1},{4,6},{5,7},{6,4},{7,5},{8,10},{9,11},{10,... | collective-permute-start | bytes 2261000 | tf_op jit(solution)/shard_map/ppermute | solution.py:501
  433.5 30.0 %collective-permute-start.11 = (bf16[8,368,128]{2,1,0:T(8,128)(2,1)S(1)}, bf16[8,368,128]{2,1,0:T(8,128)(2,1)S(1)}, u32[]{:S(2)}, u32[]{:S(2)}) collective-permute-start(bf16[8,368,128]{2,1,0:T(8,128)(2,1)S(1)} %dynamic-slice_convert_fusion.1), channel_id=1, source_target_pairs={{0,4},{4,0},{8,12},{12,8},{16,20},{20,16},{24,28},{28,24},{1,5},{5... | collective-permute-start | bytes 2261000 | tf_op jit(solution)/shard_map/ppermute | solution.py:501
  444.1 26.2 %collective-permute-start.7 = (bf16[4,368,128]{2,1,0:T(8,128)(2,1)S(1)}, bf16[4,368,128]{2,1,0:T(8,128)(2,1)S(1)}, u32[]{:S(2)}, u32[]{:S(2)}) collective-permute-start(bf16[4,368,128]{2,1,0:T(8,128)(2,1)S(1)} %dynamic-slice_convert_fusion.6), channel_id=1, source_target_pairs={{0,4},{4,0},{8,12},{12,8},{16,20},{20,16},{24,28},{28,24},{1,5},{5... | collective-permute-start | bytes 1130504 | tf_op jit(solution)/shard_map/ppermute | solution.py:501
  447.6 24.6 %collective-permute-start.2 = (bf16[4,368,128]{2,1,0:T(8,128)(2,1)S(1)}, bf16[4,368,128]{2,1,0:T(8,128)(2,1)S(1)}, u32[]{:S(2)}, u32[]{:S(2)}) collective-permute-start(bf16[4,368,128]{2,1,0:T(8,128)(2,1)S(1)} %dynamic-slice_convert_fusion.7), channel_id=1, source_target_pairs={{0,2},{1,3},{2,0},{3,1},{4,6},{5,7},{6,4},{7,5},{8,10},{9,11},{10,... | collective-permute-start | bytes 1130504 | tf_op jit(solution)/shard_map/ppermute | solution.py:501
  460.2 14.0 %collective-permute-start.17 = (bf16[4,368,128]{2,1,0:T(8,128)(2,1)S(1)}, bf16[4,368,128]{2,1,0:T(8,128)(2,1)S(1)}, u32[]{:S(2)}, u32[]{:S(2)}) collective-permute-start(bf16[4,368,128]{2,1,0:T(8,128)(2,1)S(1)} %dynamic-slice_convert_fusion.4), channel_id=1, source_target_pairs={{0,4},{4,0},{8,12},{12,8},{16,20},{20,16},{24,28},{28,24},{1,5},{5... | collective-permute-start | bytes 1130504 | tf_op jit(solution)/shard_map/ppermute | solution.py:501
  463.7 12.5 %collective-permute-start.12 = (bf16[4,368,128]{2,1,0:T(8,128)(2,1)S(1)}, bf16[4,368,128]{2,1,0:T(8,128)(2,1)S(1)}, u32[]{:S(2)}, u32[]{:S(2)}) collective-permute-start(bf16[4,368,128]{2,1,0:T(8,128)(2,1)S(1)} %dynamic-slice_convert_fusion.5), channel_id=1, source_target_pairs={{0,2},{1,3},{2,0},{3,1},{4,6},{5,7},{6,4},{7,5},{8,10},{9,11},{10,... | collective-permute-start | bytes 1130504 | tf_op jit(solution)/shard_map/ppermute | solution.py:501
  470.4 10.5 %collective-permute-start.8 = (bf16[2,368,128]{2,1,0:T(8,128)(2,1)S(1)}, bf16[2,368,128]{2,1,0:T(8,128)(2,1)S(1)}, u32[]{:S(2)}, u32[]{:S(2)}) collective-permute-start(bf16[2,368,128]{2,1,0:T(8,128)(2,1)S(1)} %dynamic-slice_convert_fusion.10), channel_id=1, source_target_pairs={{0,8},{4,12},{8,0},{12,4},{16,24},{20,28},{24,16},{28,20},{1,9},{5... | collective-permute-start | bytes 565256 | tf_op jit(solution)/shard_map/ppermute | solution.py:501
  472.3 10.6 %collective-permute-start.3 = (bf16[2,368,128]{2,1,0:T(8,128)(2,1)S(1)}, bf16[2,368,128]{2,1,0:T(8,128)(2,1)S(1)}, u32[]{:S(2)}, u32[]{:S(2)}) collective-permute-start(bf16[2,368,128]{2,1,0:T(8,128)(2,1)S(1)} %dynamic-slice_convert_fusion.11), channel_id=1, source_target_pairs={{0,8},{4,12},{8,0},{12,4},{16,24},{20,28},{24,16},{28,20},{1,9},{5... | collective-permute-start | bytes 565256 | tf_op jit(solution)/shard_map/ppermute | solution.py:501
  474.4 11.1 %collective-permute-start.18 = (bf16[2,368,128]{2,1,0:T(8,128)(2,1)S(1)}, bf16[2,368,128]{2,1,0:T(8,128)(2,1)S(1)}, u32[]{:S(2)}, u32[]{:S(2)}) collective-permute-start(bf16[2,368,128]{2,1,0:T(8,128)(2,1)S(1)} %dynamic-slice_convert_fusion.8), channel_id=1, source_target_pairs={{0,8},{4,12},{8,0},{12,4},{16,24},{20,28},{24,16},{28,20},{1,9},{5... | collective-permute-start | bytes 565256 | tf_op jit(solution)/shard_map/ppermute | solution.py:501
  476.3 13.6 %collective-permute-start.13 = (bf16[2,368,128]{2,1,0:T(8,128)(2,1)S(1)}, bf16[2,368,128]{2,1,0:T(8,128)(2,1)S(1)}, u32[]{:S(2)}, u32[]{:S(2)}) collective-permute-start(bf16[2,368,128]{2,1,0:T(8,128)(2,1)S(1)} %dynamic-slice_convert_fusion.9), channel_id=1, source_target_pairs={{0,8},{4,12},{8,0},{12,4},{16,24},{20,28},{24,16},{28,20},{1,9},{5... | collective-permute-start | bytes 565256 | tf_op jit(solution)/shard_map/ppermute | solution.py:501
  481.0 9.4 %collective-permute-start.9 = (bf16[1,368,128]{2,1,0:T(8,128)(2,1)S(1)}, bf16[1,368,128]{2,1,0:T(8,128)(2,1)S(1)}, u32[]{:S(2)}, u32[]{:S(2)}) collective-permute-start(bf16[1,368,128]{2,1,0:T(8,128)(2,1)S(1)} %dynamic-slice_convert_fusion.14), channel_id=1, source_target_pairs={{0,16},{4,20},{8,24},{12,28},{16,0},{20,4},{24,8},{28,12},{1,17},{... | collective-permute-start | bytes 282632 | tf_op jit(solution)/shard_map/ppermute | solution.py:501
  483.0 7.4 %collective-permute-start.4 = (bf16[1,368,128]{2,1,0:T(8,128)(2,1)S(1)}, bf16[1,368,128]{2,1,0:T(8,128)(2,1)S(1)}, u32[]{:S(2)}, u32[]{:S(2)}) collective-permute-start(bf16[1,368,128]{2,1,0:T(8,128)(2,1)S(1)} %dynamic-slice_convert_fusion.15), channel_id=1, source_target_pairs={{0,16},{4,20},{8,24},{12,28},{16,0},{20,4},{24,8},{28,12},{1,17},{... | collective-permute-start | bytes 282632 | tf_op jit(solution)/shard_map/ppermute | solution.py:501
  485.5 8.2 %collective-permute-start.19 = (bf16[1,368,128]{2,1,0:T(8,128)(2,1)S(1)}, bf16[1,368,128]{2,1,0:T(8,128)(2,1)S(1)}, u32[]{:S(2)}, u32[]{:S(2)}) collective-permute-start(bf16[1,368,128]{2,1,0:T(8,128)(2,1)S(1)} %dynamic-slice_convert_fusion.12), channel_id=1, source_target_pairs={{0,16},{4,20},{8,24},{12,28},{16,0},{20,4},{24,8},{28,12},{1,17},{... | collective-permute-start | bytes 282632 | tf_op jit(solution)/shard_map/ppermute | solution.py:501
  490.1 5.6 %collective-permute-start.14 = (bf16[1,368,128]{2,1,0:T(8,128)(2,1)S(1)}, bf16[1,368,128]{2,1,0:T(8,128)(2,1)S(1)}, u32[]{:S(2)}, u32[]{:S(2)}) collective-permute-start(bf16[1,368,128]{2,1,0:T(8,128)(2,1)S(1)} %dynamic-slice_convert_fusion.13), channel_id=1, source_target_pairs={{0,16},{4,20},{8,24},{12,28},{16,0},{20,4},{24,8},{28,12},{1,17},{... | collective-permute-start | bytes 282632 | tf_op jit(solution)/shard_map/ppermute | solution.py:501
  (17 other events, 65.2 us)
Sparse Core Ops, SparseCore 0:
  11.5 70.7 all-gather.4
  85.8 67.0 all-gather.2
where the time goes:
time: 516 us; the launch traced here: 507 us
  Pallas kernels  204 us (40%)
  waiting for transfers between devices  184 us (36%)
  local copies, waits for them, and re-layouts  42.6 us (8%)
  other arithmetic  30 us (6%)
  starting transfers between devices  26.3 us (5%)
  between operations  16.6 us (3%)
    all_gather x2, waiting for transfers between devices, shards(): gathered.append(lax.all_gather(own, (DP, FSDP), axis=0, tiled=True))  129 us
    pallas_call x2, Pallas kernels, attn_bwd(): call(attn_bwd_body, (sds((CELLS, D), F32), sds((D, 3 * D), F32), sds((D,...  53.6 us
    ppermute x20, waiting for transfers between devices, halve(): got = lax.ppermute(send, axis, flip_pairs(axis, bit))  45.9 us
    pallas_call x2, Pallas kernels, attn_fwd(): call(attn_fwd_body, (sds((CELLS, D), F32), sds((WTOK, D), BF), sds((WTOK,...  39.7 us
    pallas_call x2, Pallas kernels, moe_bwd(): call(moe_bwd_body, (sds((CELLS, D), F32), sds((EXPERTS, D, F), F32), sds(...  36.5 us
    pallas_call x2, Pallas kernels, moe_fwd(): call(moe_fwd_body, (sds((CELLS, D), out_dtype), sds((CELLS, D), BF), sds(...  29.8 us
    pallas_call x2, Pallas kernels, unpack_weights(): call(functools.partial(unpack_body, rows, devices, padded), (sds((D, 3 *...  25.7 us
    pallas_call x2, Pallas kernels, pack_grads(): call(functools.partial(pack_body, rows, devices, padded, orders), (sds((d...  18.9 us
  transfers between devices with their start and end apart: 27, of which 18 were waited for; matrix products, arithmetic and copies ran while one was open for 8% of the time, Pallas kernels for 4%

commit v1 on v0

v1 whole, which is shorter than its diff:
```python
import functools
import math
from typing import Any, NamedTuple

import jax
import jax.numpy as jnp
import numpy as np
from jax import lax
from jax.experimental import pallas as pl
from jax.experimental.pallas import tpu as pltpu
from jax.sharding import PartitionSpec as P

D = 384
HEADS = 12
F = 1536
HEAD_DIM = 32
EXPERTS = 2
CAP = 256
SIDE = 28
WIN = 7
SHIFT = 3
BLOCKS = 2
CELLS = 784
GROUP = 392
RELS = 169
NORM_EPSILON = 1e-05
MOMENTUM_DECAY = 0.9
AVERAGE_DECAY = 0.9
RATE_BASE = 0.1

DP = "dp"
FSDP = "fsdp"
LANES = 128
WROWS = 64
WINDOWS = 16
WTOK = WINDOWS * WROWS
SLOTS = EXPERTS * 2 * CAP
PAIR = 4 * WROWS
QUADS = HEADS // 4
SCALE = HEAD_DIM ** (-0.5)
US_FLOPS = 1.1e9
BF = jnp.bfloat16
F32 = jnp.float32
VMEM_BYTES = 20 * 1024 * 1024


def call(body, out_shape, n_in, scratch=(), smem=0, deps=(), us=1, vmem=VMEM_BYTES):
    def skipping(*refs):
        body(*refs[:n_in], *refs[n_in + len(deps) :])

    run = pl.pallas_call(
        skipping,
        out_shape=out_shape,
        in_specs=[pl.BlockSpec(memory_space=pltpu.SMEM)] * smem
        + [pl.BlockSpec(memory_space=pltpu.VMEM)] * (n_in - smem)
        + [pl.BlockSpec(memory_space=pl.ANY)] * len(deps),
        out_specs=jax.tree.map(lambda _: pl.BlockSpec(memory_space=pltpu.VMEM), out_shape),
        scratch_shapes=list(scratch),
        compiler_params=pltpu.CompilerParams(vmem_limit_bytes=vmem),
        cost_estimate=pl.CostEstimate(flops=int(us * US_FLOPS), bytes_accessed=0, transcendentals=0),
    )
    return lambda *args: run(*args, *deps)


def sds(shape, dtype):
    return jax.ShapeDtypeStruct(shape, dtype)


def nn(a, b):
    return lax.dot_general(a, b, (((1,), (0,)), ((), ())), preferred_element_type=F32)


def nt(a, b):
    return lax.dot_general(a, b, (((1,), (1,)), ((), ())), preferred_element_type=F32)


def tn(a, b):
    return lax.dot_general(a, b, (((0,), (0,)), ((), ())), preferred_element_type=F32)


def normalize(hidden):
    centre = hidden - jnp.mean(hidden, axis=-1, keepdims=True)
    inverse = lax.rsqrt(jnp.mean(centre * centre, axis=-1, keepdims=True) + NORM_EPSILON)
    return centre * inverse, inverse


def norm_backward(grad_normed, normal_rows, inverse, gain_row):
    scaled = grad_normed * gain_row
    return inverse * (
        scaled
        - jnp.mean(scaled, axis=-1, keepdims=True)
        - normal_rows * jnp.mean(scaled * normal_rows, axis=-1, keepdims=True)
    )


def head_masks():
    lane = lax.broadcasted_iota(jnp.int32, (1, LANES), 1) // HEAD_DIM
    return [lane == h for h in range(4)]


def stack_heads(rows, masks):
    zero = jnp.zeros_like(rows)
    return jnp.concatenate([jnp.where(mask, rows, zero) for mask in masks], axis=0)


def fold_heads(tall, masks):
    out = jnp.where(masks[0], tall[0:WROWS], 0.0)
    for h in range(1, 4):
        out = jnp.where(masks[h], tall[h * WROWS : (h + 1) * WROWS], out)
    return out


def patch_of(row, shifted):
    w, p = row >> 6, row & 63
    pr = (p * 37) >> 8
    r = (w >> 2) * WIN + pr
    s = (w & 3) * WIN + p - pr * WIN
    if shifted:
        r, s = r + SHIFT, s + SHIFT
        r = jnp.where(r >= SIDE, r - SIDE, r)
        s = jnp.where(s >= SIDE, s - SIDE, s)
    return jnp.where(p < WIN * WIN, r * SIDE + s, -1)


def fill_perm(perm, shifted):
    @pl.loop(0, 8)
    def _(t):
        row = lax.broadcasted_iota(jnp.int32, (128, 1), 0) + t * 128
        same = patch_of(row, shifted) == lax.broadcasted_iota(jnp.int32, (128, CELLS), 1)
        perm[pl.ds(pl.multiple_of(t * 128, 128), 128), :] = jnp.where(same, 1.0, 0.0).astype(BF)


def fill_perm_t(perm_t, shifted):
    source = patch_of(lax.broadcasted_iota(jnp.int32, (1, WTOK), 1), shifted)

    @pl.loop(0, 7)
    def _(t):
        row = lax.broadcasted_iota(jnp.int32, (112, WTOK), 0) + t * 112
        perm_t[pl.ds(pl.multiple_of(t * 112, 112), 112), :] = jnp.where(row == source, 1.0, 0.0).astype(BF)


def fill_slots(onehot, onehot_t, place_col, place_row):
    @pl.loop(0, 7)
    def _(t):
        rows = pl.ds(pl.multiple_of(t * 112, 112), 112)
        place = jnp.concatenate([place_col[rows, :]] * 8, axis=1)
        same = place == lax.broadcasted_iota(jnp.int32, (112, SLOTS), 1)
        onehot[rows, :] = jnp.where(same, 1.0, 0.0).astype(BF)

    @pl.loop(0, 8)
    def _(t):
        row = lax.broadcasted_iota(jnp.int32, (128, CELLS), 0) + t * 128
        same = row == place_row[0:1, :]
        onehot_t[pl.ds(pl.multiple_of(t * 128, 128), 128), :] = jnp.where(same, 1.0, 0.0).astype(BF)


PERM = pltpu.VMEM((WTOK, CELLS), BF)
PERM_T = pltpu.VMEM((CELLS, WTOK), BF)


def attn_fwd_body(shifted, hid, vec, w_in, w_out, bias, mask, h_one, wn, qkv, mixed, attn, perm, perm_t):
    fill_perm(perm, shifted)
    fill_perm_t(perm_t, shifted)
    normal, _ = normalize(hid[...].astype(F32))
    normed = (normal * vec[0:1] + vec[1:2]).astype(BF)
    wn[...] = nn(perm[...], normed).astype(BF)
    in_bias = jnp.concatenate([vec[4:5], jnp.zeros((1, D), F32), vec[5:6]], axis=1)

    @pl.loop(0, 4)
    def _(t):
        rows = pl.ds(pl.multiple_of(t * 256, 256), 256)
        qkv[rows, :] = (nn(wn[rows, :], w_in[...]) + in_bias).astype(BF)

    masks = head_masks()

    @pl.loop(0, WINDOWS)
    def _(w):
        rows = pl.ds(pl.multiple_of(w * WROWS, WROWS), WROWS)
        allow = mask[w] > 0.0
        allow = jnp.concatenate([allow, allow], axis=1)
        for g in range(QUADS):
            cols = slice(g * LANES, (g + 1) * LANES)
            q4 = stack_heads(qkv[rows, g * LANES : (g + 1) * LANES], masks)
            kg = qkv[rows, D + g * LANES : D + (g + 1) * LANES]
            vg = qkv[rows, 2 * D + g * LANES : 2 * D + (g + 1) * LANES]
            s = jnp.where(allow, nt(kg, q4) * SCALE + bias[g], -1e30)
            e = jnp.exp(s - jnp.max(s, axis=0, keepdims=True))
            a = e * (1.0 / jnp.sum(e, axis=0, keepdims=True))
            a = a.astype(BF)
            attn[w * QUADS + g] = a
            mixed[rows, cols] = fold_heads(tn(a, vg), masks).astype(BF)

    back = nn(perm_t[...], mixed[...]).astype(BF)
    h_one[...] = hid[...].astype(F32) + nn(back, w_out[...]) + vec[6:7]


def attn_fwd(shifted, hid, vec, w_in, w_out, bias, mask, deps=()):
    return call(
        functools.partial(attn_fwd_body, shifted),
        (
            sds((CELLS, D), F32),
            sds((WTOK, D), BF),
            sds((WTOK, 3 * D), BF),
            sds((WTOK, D), BF),
            sds((WINDOWS * QUADS, WROWS, PAIR), BF),
        ),
        6,
        scratch=[PERM, PERM_T],
        us=17,
        deps=deps,
    )(hid, vec, w_in, w_out, bias, mask)


def moe_fwd_body(
    h_one, vec, w1, w2, b1, router, router_bias, place_col, place_row,
    out, normed_two, disp, act, slope, picked, gap_out, rows_out, onehot, onehot_t,
):
    fill_slots(onehot, onehot_t, place_col, place_row)
    normal, _ = normalize(h_one[...])
    two = (normal * vec[2:3] + vec[3:4]).astype(BF)
    normed_two[...] = two
    logits = nn(two, router[...])
    gap = (logits[:, LANES:] + router_bias[1:2]) - (logits[:, :LANES] + router_bias[0:1])
    gap = jnp.where(place_col[...] >= SLOTS // 2, gap, -gap)
    gap_out[...] = gap
    gate = 1.0 / (1.0 + jnp.exp(-gap))
    disp[...] = nn(onehot_t[...], two).astype(BF)

    @pl.loop(0, 4)
    def _(t):
        rows = pl.ds(pl.multiple_of(t * 256, 256), 256)
        e = t // 2
        own = disp[rows, :]
        for c in range(3):
            cols = slice(c * 512, (c + 1) * 512)
            pre = nn(own, w1[e, :, cols]) + b1[pl.ds(e, 1), cols]
            phi = 0.5 * (1.0 + lax.erf(pre * 0.7071067811865476))
            act[rows, cols] = (pre * phi).astype(BF)
            slope[rows, cols] = (
                phi + pre * jnp.exp(-0.5 * pre * pre) * 0.3989422804014327
            ).astype(BF)
        rows_out[rows, :] = (nn(act[rows, :], w2[e]) + vec[pl.ds(7 + e, 1)]).astype(BF)

    taken = nn(onehot[...], rows_out[...])
    picked[...] = taken.astype(BF)
    for c in range(3):
        cols = slice(c * LANES, (c + 1) * LANES)
        out[:, cols] = (h_one[:, cols] + gate * taken[:, cols]).astype(out.dtype)


def moe_fwd(h_one, vec, w1, w2, b1, router, router_bias, place, out_dtype, deps=()):
    return call(
        moe_fwd_body,
        (
            sds((CELLS, D), out_dtype),
            sds((CELLS, D), BF),
            sds((SLOTS, D), BF),
            sds((SLOTS, F), BF),
            sds((SLOTS, F), BF),
            sds((CELLS, D), BF),
            sds((CELLS, LANES), F32),
        ),
        9,
        scratch=[pltpu.VMEM((SLOTS, D), BF), PERM_T, PERM],
        us=9.5,
        deps=deps,
    )(h_one, vec, w1, w2, b1, router, router_bias, *place)


def moe_bwd_body(
    grad, h_one, vec, w1, w2, place_col, place_row,
    normed_two, disp, act, slope, picked, gap,
    grad_one, dw1, dw2, db1, drouter, small, g_rows, g_pre, g_disp, onehot, onehot_t,
):
    fill_slots(onehot, onehot_t, place_col, place_row)
    go = grad[...].astype(F32)
    gate = 1.0 / (1.0 + jnp.exp(-gap[...]))
    other = 1.0 / (1.0 + jnp.exp(gap[...]))
    gate_wide = jnp.concatenate([gate] * 3, axis=1)
    g_picked = (go * gate_wide).astype(BF)
    g_gate = jnp.sum(go * picked[...].astype(F32), axis=-1, keepdims=True)
    sign = jnp.where(place_col[...] >= SLOTS // 2, 1.0, -1.0)
    gl = (g_gate * gate * other * sign).astype(BF).astype(F32)
    g_rows[...] = nn(onehot_t[...], g_picked).astype(BF)

    @pl.loop(0, EXPERTS)
    def _(e):
        total = jnp.zeros((1, F), F32)
        for t in range(2):
            rows = pl.ds(pl.multiple_of(e * 512 + t * 256, 256), 256)
            own = g_rows[rows, :]
            parts = []
            for c in range(3):
                cols = slice(c * 512, (c + 1) * 512)
                gp = (nt(own, w2[e, cols, :]) * slope[rows, cols].astype(F32)).astype(BF)
                g_pre[t * 256 : (t + 1) * 256, cols] = gp
                parts.append(jnp.sum(gp.astype(F32), axis=0, keepdims=True))
            total = total + jnp.concatenate(parts, axis=1)
            g_disp[rows, :] = nt(g_pre[t * 256 : (t + 1) * 256, :], w1[e]).astype(BF)
        db1[pl.ds(e, 1), :] = total
        both = pl.ds(pl.multiple_of(e * 512, 512), 512)
        small[pl.ds(7 + e, 1), :] = jnp.sum(g_rows[both, :].astype(F32), axis=0, keepdims=True)
        for c in range(3):
            cols = slice(c * 512, (c + 1) * 512)
            dw1[e, :, cols] = tn(disp[both, :], g_pre[:, cols])
            dw2[e, cols, :] = tn(act[both, cols], g_rows[both, :])

    g_two = nn(onehot[...], g_disp[...])
    gl_wide = jnp.concatenate([gl] * 3, axis=1)
    g_two = g_two + gl_wide * vec[9:10]
    drouter[...] = tn(gl.astype(BF), normed_two[...])[0:8]
    normal, inverse = normalize(h_one[...])
    small[0:1] = jnp.zeros((1, D), F32)
    small[1:2] = jnp.zeros((1, D), F32)
    small[2:3] = jnp.sum(g_two * normal, axis=0, keepdims=True)
    small[3:4] = jnp.sum(g_two, axis=0, keepdims=True)
    small[4:7] = jnp.zeros((3, D), F32)
    small[9:16] = jnp.zeros((7, D), F32)
    small[9:10] = jnp.sum(gl_wide, axis=0, keepdims=True)
    grad_one[...] = go + norm_backward(g_two, normal, inverse, vec[2:3])


def moe_bwd(grad, h_one, vec, w1, w2, place, saved, deps=()):
    return call(
        moe_bwd_body,
        (
            sds((CELLS, D), F32),
            sds((EXPERTS, D, F), F32),
            sds((EXPERTS, F, D), F32),
            sds((8, F), F32),
            sds((8, D), F32),
            sds((16, D), F32),
        ),
        13,
        scratch=[
            pltpu.VMEM((SLOTS, D), BF),
            pltpu.VMEM((512, F), BF),
            pltpu.VMEM((SLOTS, D), BF),
            PERM_T,
            PERM,
        ],
        us=10.5,
        deps=deps,
    )(grad, h_one, vec, w1, w2, *place, *saved)


def attn_bwd_body(
    shifted, grad_one, w_out, qkv, mixed, attn,
    g_qkv, dw_out, dbias, small, g_mix, perm,
):
    fill_perm(perm, shifted)
    gao = grad_one[...].astype(BF)
    small[...] = jnp.zeros((16, D), F32)
    small[6:7] = jnp.sum(gao.astype(F32), axis=0, keepdims=True)
    gao_w = nn(perm[...], gao).astype(BF)
    dw_out[...] = tn(mixed[...], gao_w)
    g_mix[...] = nt(gao_w, w_out[...]).astype(BF)
    dbias[...] = jnp.zeros_like(dbias)
    masks = head_masks()

    @pl.loop(0, WINDOWS)
    def _(w):
        rows = pl.ds(pl.multiple_of(w * WROWS, WROWS), WROWS)
        for g in range(QUADS):
            cols = slice(g * LANES, (g + 1) * LANES)
            kcols = slice(D + g * LANES, D + (g + 1) * LANES)
            vcols = slice(2 * D + g * LANES, 2 * D + (g + 1) * LANES)
            q4 = stack_heads(qkv[rows, cols], masks)
            kg = qkv[rows, kcols]
            vg = qkv[rows, vcols]
            d4 = stack_heads(g_mix[rows, cols], masks)
            a = attn[w * QUADS + g]
            a32 = a.astype(F32)
            t = a32 * nt(vg, d4)
            ds = (t - a32 * jnp.sum(t, axis=0, keepdims=True)).astype(BF)
            dbias[g] += ds.astype(F32)
            g_qkv[rows, cols] = (fold_heads(tn(ds, kg), masks) * SCALE).astype(BF)
            g_qkv[rows, kcols] = (nn(ds, q4) * SCALE).astype(BF)
            g_qkv[rows, vcols] = nn(a, d4).astype(BF)

    small[4:5] = jnp.sum(g_qkv[:, :D].astype(F32), axis=0, keepdims=True)
    small[5:6] = jnp.sum(g_qkv[:, 2 * D :].astype(F32), axis=0, keepdims=True)


def attn_bwd(shifted, grad_one, w_out, saved, deps=()):
    return call(
        functools.partial(attn_bwd_body, shifted),
        (
            sds((WTOK, 3 * D), BF),
            sds((D, D), F32),
            sds((QUADS, WROWS, PAIR), F32),
            sds((16, D), F32),
        ),
        5,
        scratch=[pltpu.VMEM((WTOK, D), BF), PERM],
        us=16.5,
        deps=deps,
    )(grad_one, w_out, *saved)


def proj_bwd_body(shifted, grad_one, hid, vec, w_in, wn, g_qkv, grad_in, dw_in, small, perm_t):
    fill_perm_t(perm_t, shifted)
    for c in range(3):
        cols = slice(c * D, (c + 1) * D)
        dw_in[:, cols] = tn(wn[...], g_qkv[:, cols])
    g_flat = nn(perm_t[...], g_qkv[...]).astype(BF)
    g_normed = nt(g_flat, w_in[...])
    normal, inverse = normalize(hid[...].astype(F32))
    small[...] = jnp.zeros((16, D), F32)
    small[0:1] = jnp.sum(g_normed * normal, axis=0, keepdims=True)
    small[1:2] = jnp.sum(g_normed, axis=0, keepdims=True)
    grad_in[...] = grad_one[...] + norm_backward(g_normed, normal, inverse, vec[0:1])


def proj_bwd(shifted, grad_one, hid, vec, w_in, wn, g_qkv, deps=()):
    return call(
        functools.partial(proj_bwd_body, shifted),
        (sds((CELLS, D), F32), sds((D, 3 * D), F32), sds((16, D), F32)),
        6,
        scratch=[PERM_T],
        us=5.5,
        deps=deps,
    )(grad_one, hid, vec, w_in, wn, g_qkv)


def window_perm_t(shifted):
    source = patch_of(jnp.arange(WTOK, dtype=jnp.int32), shifted)
    return (jnp.arange(CELLS, dtype=jnp.int32)[:, None] == source[None, :]).astype(BF)


def wrap_codes(shifted):
    code = np.zeros((CELLS,), np.float32)
    if shifted:
        for r in range(SIDE):
            for s in range(SIDE):
                rr, ss = (r - SHIFT) % SIDE, (s - SHIFT) % SIDE
                code[r * SIDE + s] = 2 * (rr >= SIDE - SHIFT) + (ss >= SIDE - SHIFT)
    return code


def window_masks(items, shifted):
    labels = items.astype(F32)
    if shifted:
        labels = labels * 4.0 + jnp.asarray(wrap_codes(True))
    placed = nn(jnp.broadcast_to((labels + 1.0).astype(BF), (8, CELLS)), window_perm_t(shifted))[0]
    placed = placed.reshape(WINDOWS, WROWS)
    same = (placed[:, :, None] == placed[:, None, :]) & (placed[:, :, None] > 0.0)
    same = same.astype(F32)
    return jnp.concatenate([same, same], axis=2)


def slot_places(routes, slots):
    group = (jnp.arange(CELLS, dtype=jnp.int32) // GROUP) * CAP
    place = routes * (2 * CAP) + group + slots
    return jnp.broadcast_to(place[:, None], (CELLS, LANES)), jnp.broadcast_to(place[None, :], (8, CELLS))

LEAD = 73
SMALL = 9326
LAG = LEAD * LANES - SMALL
SPANS = ((LEAD, D, 9), (LEAD + 3456, D, 3), (LEAD + 4608, 2 * D, 12), (LEAD + 4608 + 9216, 2 * F, 3))
ALIGNED = LEAD + 4608 + 2 * 9216


def relative(k, bits):
    total = 0
    for place, bit in enumerate(bits):
        total = total + (((k >> (len(bits) - 1 - place)) & 1) << bit)
    return total


def lanes_of(count=LANES):
    return lax.broadcasted_iota(jnp.int32, (1, count), 1)


def equal(rows, columns):
    return jnp.where(rows == columns, 1.0, 0.0).astype(BF)


def spread(shape):
    return lax.broadcasted_iota(jnp.int32, shape, 0), lax.broadcasted_iota(jnp.int32, shape, 1)


def exact(left, one, product):
    high = left.astype(BF)
    low = (left - high.astype(F32)).astype(BF)
    return product(high, one) + product(low, one)


def head_major():
    f, g = spread((D, D))
    return equal(f, 12 * (g & 31) + (g >> 5))


def head_rows(m):
    f, g = spread((D, 2 * LANES))
    return equal((f & 31) + 32 * m, g)


def offset_lanes():
    f, g = spread((LANES, LANES))
    i = g & 63
    r = (i * 37) >> 8
    return equal(f, jnp.where(i < WIN * WIN, 13 * r + i - WIN * r, -1))


def turns():
    return [13 * (6 - j // WIN) + 6 - j % WIN for j in range(WIN * WIN)]


def unpack_bias(flat, wide, tall, bias):
    wide[...] = jnp.zeros_like(wide)
    for m in range(6):
        for c in range(3):
            wide[m : m + 1, c * LANES : (c + 1) * LANES] = flat[12 + 3 * m + c : 13 + 3 * m + c, :]
    by_head = nn(wide[...].astype(BF), head_major())
    sub = lax.broadcasted_iota(jnp.int32, (16, D), 0)
    own = (lanes_of(D) >> 5) == sub
    table = jnp.zeros((16, 2 * LANES), F32)
    for m in range(6):
        table = table + nn(jnp.where(own, by_head[m : m + 1], 0.0).astype(BF), head_rows(m))
    tall[...] = jnp.zeros_like(tall)
    for j, turn in enumerate(turns()):
        row = pltpu.roll(table, (2 * LANES - turn) % (2 * LANES), 1)[:, :LANES]
        tall[pl.ds(j, 16, stride=WROWS), :] = row
    tall[...] = nn(tall[...].astype(BF), offset_lanes())
    for g in range(QUADS):
        for t in range(2):
            h = 4 * g + 2 * t
            left, right = tall[h * WROWS : (h + 1) * WROWS], tall[(h + 1) * WROWS : (h + 2) * WROWS]
            bias[g, :, t * LANES : (t + 1) * LANES] = jnp.where(lanes_of() < WROWS, left, right)


def unpack_small(flat, rows, wide, tall, vec, b1, router, router_bias, bias):
    def shifted(first, count, by):
        near, far = flat[first : first + count, :], flat[first + 1 : first + 1 + count, :]
        return pltpu.roll(jnp.where(lanes_of() >= by, near, far), LANES - by, 1)

    rows[0:16, :] = shifted(27, 16, 108)
    rows[16:46, :] = shifted(42, 30, 110)
    vec[...] = jnp.zeros_like(vec)
    b1[...] = jnp.zeros_like(b1)
    for c in range(3):
        cols = slice(c * LANES, (c + 1) * LANES)
        for n in range(4):
            vec[n : n + 1, cols] = flat[3 * n + c : 3 * n + c + 1, :]
        for n in range(3):
            vec[4 + n : 5 + n, cols] = rows[3 * n + c : 3 * n + c + 1, :]
        for e in range(EXPERTS):
            vec[7 + e : 8 + e, cols] = rows[40 + 3 * e + c : 41 + 3 * e + c, :]
    for e in range(EXPERTS):
        for c in range(12):
            b1[e : e + 1, c * LANES : (c + 1) * LANES] = rows[16 + 12 * e + c : 17 + 12 * e + c, :]
        one = jnp.sum(jnp.where(lanes_of() == e, rows[15:16, :], 0.0), axis=1, keepdims=True)
        router_bias[e : e + 1, :] = jnp.broadcast_to(one, (1, LANES))
    pairs = jnp.concatenate([rows[9 + c : 10 + c, :] for c in range(6)], axis=1)
    pairs = jnp.broadcast_to(pairs, (LANES, 2 * D)).astype(BF)
    d, f = spread((D, 2 * D))
    for e in range(EXPERTS):
        router[:, e * LANES : (e + 1) * LANES] = nt(equal(f, 2 * d + e), pairs).astype(BF)
    gap = nt(pairs[0:16], equal(f, 2 * d + 1)) - nt(pairs[0:16], equal(f, 2 * d))
    vec[9:10, :] = gap[0:1]
    unpack_bias(flat, wide, tall, bias)


def unpack_body(rows, padded, runs, me, *refs):
    got = refs[: len(runs)]
    w_in, w_out, w1, w2, vec, b1, router, router_bias, bias, flat, few, wide, tall = refs[len(runs) :]
    for (bits, fixed), part in zip(runs, got):

        @pl.loop(0, 1 << len(bits))
        def _(k, bits=bits, fixed=fixed, part=part):
            d = me[0] ^ (relative(k, bits) + fixed)
            flat[pl.ds(d * rows, rows), :] = part[k, :rows, :].astype(F32)

    unpack_small(flat, few, wide, tall, vec, b1, router, router_bias, bias)
    for (base, height, tiles), out in zip(SPANS, (w_in, w_out, w1, w2)):
        step = 64

        @pl.loop(0, height // step)
        def _(t, base=base, tiles=tiles, out=out):
            first = base - 1 + t * (step * tiles)
            before = flat[pl.ds(first, step, stride=tiles), :]
            for j in range(tiles):
                here = flat[pl.ds(first + 1 + j, step, stride=tiles), :]
                tile = pltpu.roll(jnp.where(lanes_of() >= LANES - LAG, before, here), LAG, 1)
                out[pl.ds(pl.multiple_of(t * step, step), step), j * LANES : (j + 1) * LANES] = tile.astype(BF)
                before = here


class Weights(NamedTuple):
    w_in: Any
    w_out: Any
    w1: Any
    w2: Any
    vec: Any
    b1: Any
    router: Any
    router_bias: Any
    bias: Any


def unpack_weights(me, parts, runs, rows, devices, deps=()):
    padded = parts[0].shape[1]
    got = Weights(
        *call(
            functools.partial(unpack_body, rows, padded, runs),
            (
                sds((D, 3 * D), BF),
                sds((D, D), BF),
                sds((2 * D, F), BF),
                sds((2 * F, D), BF),
                sds((16, D), F32),
                sds((8, F), F32),
                sds((D, 2 * LANES), BF),
                sds((8, LANES), F32),
                sds((QUADS, WROWS, PAIR), F32),
            ),
            1 + len(parts),
            scratch=[
                pltpu.VMEM((devices * rows + 8, LANES), F32),
                pltpu.VMEM((48, LANES), F32),
                pltpu.VMEM((8, D), F32),
                pltpu.VMEM((16 * WROWS, LANES), F32),
            ],
            smem=1,
            us=10,
            deps=deps,
        )(me, *parts)
    )
    return got._replace(w1=got.w1.reshape(EXPERTS, D, F), w2=got.w2.reshape(EXPERTS, F, D))


def pack_bias(dbias, wide, tall):
    tall[HEADS * WROWS :, :] = jnp.zeros((4 * WROWS, LANES), F32)
    for h in range(HEADS):
        g, t, side = h // 4, (h % 4) // 2, h % 2
        tile = dbias[g, :, t * LANES : (t + 1) * LANES]
        tall[h * WROWS : (h + 1) * WROWS, :] = jnp.where((lanes_of() >> 6) == side, tile, 0.0)
    used = HEADS * WROWS
    tall[0:used, :] = exact(tall[0:used, :], offset_lanes(), nt)
    table = jnp.zeros((16, 2 * LANES), F32)
    for j, turn in enumerate(turns()):
        row = tall[pl.ds(j, 16, stride=WROWS), :]
        table = table + pltpu.roll(jnp.concatenate([row, jnp.zeros_like(row)], axis=1), turn, 1)
    sub = lax.broadcasted_iota(jnp.int32, (16, D), 0)
    own = (lanes_of(D) >> 5) == sub
    wide[...] = jnp.zeros_like(wide)
    for m in range(6):
        placed = jnp.where(own, exact(table, head_rows(m), nt), 0.0)
        wide[m : m + 1, :] = jnp.sum(placed, axis=0, keepdims=True)
    wide[...] = exact(wide[...], head_major(), nt)


def pack_small(al, vectors, drouter, db1, dbias, one, two, wide, tall):
    one[...] = jnp.zeros_like(one)
    two[...] = jnp.zeros_like(two)
    pack_bias(dbias, wide, tall)
    d, f = spread((D, 2 * D))
    signs = equal(f, 2 * d + 1) - equal(f, 2 * d)
    pairs = exact(drouter[...], signs, nn)
    for c in range(3):
        cols = slice(c * LANES, (c + 1) * LANES)
        for n in range(4):
            one[1 + 3 * n + c : 2 + 3 * n + c, :] = vectors[n : n + 1, cols]
        for m in range(6):
            one[13 + 3 * m + c : 14 + 3 * m + c, :] = wide[m : m + 1, cols]
        for n in range(3):
            two[1 + 3 * n + c : 2 + 3 * n + c, :] = vectors[4 + n : 5 + n, cols]
        for e in range(EXPERTS):
            al[67 + 3 * e + c : 68 + 3 * e + c, :] = vectors[7 + e : 8 + e, cols]
    for c in range(6):
        two[10 + c : 11 + c, :] = pairs[0:1, c * LANES : (c + 1) * LANES]
    total = vectors[9:10, 0:LANES]
    two[16:17, :] = jnp.where(lanes_of() == 0, -total, jnp.where(lanes_of() == 1, total, 0.0))
    for e in range(EXPERTS):
        for c in range(12):
            al[43 + 12 * e + c : 44 + 12 * e + c, :] = db1[e : e + 1, c * LANES : (c + 1) * LANES]
    first = pltpu.roll(jnp.where(lanes_of() >= LANES - 18, one[0:28, :], one[1:29, :]), 18, 1)
    second = pltpu.roll(jnp.where(lanes_of() >= LANES - 126, two[0:16, :], two[1:17, :]), 126, 1)
    al[27:43, :] = second
    al[0:27, :] = first[0:27]
    al[27:28, :] += first[27:28]


def pack_body(
    rows, padded, runs, me, moe, attn, proj, drouter, db1, dbias, dw_in, dw_out, dw1, dw2,
    keep, send, vectors, al, one, two, wide, tall,
):
    vectors[...] = moe[...] + attn[...] + proj[...]
    pack_small(al, vectors, drouter, db1, dbias, one, two, wide, tall)
    tail = al.shape[0] - ALIGNED
    al[pl.ds(ALIGNED, tail), :] = jnp.zeros((tail, LANES), F32)
    for (base, height, tiles), grad in zip(SPANS, (dw_in, dw_out, dw1, dw2)):
        step = 64

        @pl.loop(0, height // step)
        def _(t, base=base, tiles=tiles, grad=grad):
            first = base + t * (step * tiles)
            own = pl.ds(pl.multiple_of(t * step, step), step)
            for j in range(tiles):
                al[pl.ds(first + j, step, stride=tiles), :] = grad[own, j * LANES : (j + 1) * LANES]

    at = 0
    for bits, fixed in runs:
        for other, out in enumerate((keep, send)):

            @pl.loop(0, 1 << len(bits))
            def _(k, bits=bits, fixed=fixed, at=at, other=other, out=out):
                d = me[0] ^ (relative(k, bits) + fixed + other)
                out[at + k] = al[pl.ds(d * rows, padded), :].astype(BF)

        at += 1 << len(bits)


def pack_grads(me, small, dw_in, dw_out, dw1, dw2, runs, rows, devices, padded, deps=()):
    shape = sds((devices // 2, padded, LANES), BF)
    return call(
        functools.partial(pack_body, rows, padded, runs),
        (shape, shape, sds((16, D), F32)),
        11,
        scratch=[
            pltpu.VMEM((devices * rows + padded, LANES), F32),
            pltpu.VMEM((40, LANES), F32),
            pltpu.VMEM((24, LANES), F32),
            pltpu.VMEM((8, D), F32),
            pltpu.VMEM((16 * WROWS, LANES), F32),
        ],
        smem=1,
        us=4,
        deps=deps,
    )(me, *small, dw_in, dw_out, dw1.reshape(2 * D, F), dw2.reshape(2 * F, D))


def join_body(a, b, out):
    n = a.shape[0]

    @pl.loop(0, n)
    def _(i):
        out[i] = a[i]
        out[n + i] = b[i]


def join(a, b):
    return call(join_body, sds((2 * a.shape[0], *a.shape[1:]), a.dtype), 2)(a, b)


class Ways(NamedTuple):
    core: Any
    x: Any
    y: Any
    low: Any
    high: Any
    rest: Any


def ways():
    dp, fsdp = (lax.axis_size(axis).bit_length() - 1 for axis in (DP, FSDP))
    rest = [(DP, bit) for bit in range(1, dp - 2)] + [(FSDP, bit) for bit in range(2, fsdp)]
    return Ways((FSDP, 0), (FSDP, 1), (DP, 0), (DP, dp - 2), (DP, dp - 1), rest)


def weight_bit(way):
    axis, bit = way
    return bit if axis == FSDP else bit + lax.axis_size(FSDP).bit_length() - 1


def flip(array, way):
    axis, bit = way
    return lax.ppermute(array, axis, [(i, i ^ (1 << bit)) for i in range(lax.axis_size(axis))])


def tie(arrays, others):
    return lax.optimization_barrier((arrays, others))[0]


def bits_of(*order):
    return [weight_bit(way) for way in order]


class Gather:
    def __init__(self, own, way):
        for extra in way.rest:
            own = join(own, flip(own, extra))
        self.way, self.own = way, own
        self.rest = bits_of(*reversed(way.rest))

    def far(self):
        own, way = self.own, self.way
        self.pair = join(own, flip(own, way.high))
        self.over = flip(self.pair, way.low)

    def near(self):
        way = self.way
        self.a = join(self.pair, flip(self.pair, way.x))
        self.b = join(self.over, flip(self.over, way.y))

    def last(self):
        way = self.way
        self.parts = [self.a, flip(self.a, way.y), self.b, flip(self.b, way.x)]
        self.parts += [flip(part, way.core) for part in self.parts]
        high, rest = bits_of(way.high), self.rest
        one, two = bits_of(way.x) + high + rest, bits_of(way.y) + high + rest
        x, y, low, core = (1 << weight_bit(w) for w in (way.x, way.y, way.low, way.core))
        self.runs = [(one, 0), (one, y), (two, low), (two, low + x)]
        self.runs += [(bits, fixed + core) for bits, fixed in self.runs]


def scatter_runs(way):
    tail = bits_of(way.high, *way.rest)
    x, y, low = (1 << weight_bit(w) for w in (way.x, way.y, way.low))
    bx, by = bits_of(way.x), bits_of(way.y)
    return [(bx + tail, y), (tail, x), (tail, 0), (by + tail, low + x), (tail, low + y), (tail, low)]


class Scatter:
    def __init__(self, keep, send, way):
        self.way, self.keep, self.n = way, keep, keep.shape[0] // 16
        self.got = flip(send, way.core)

    def sum(self, first, count):
        cut = slice(first * self.n, (first + count) * self.n)
        return self.keep[cut].astype(F32) + self.got[cut].astype(F32)

    def near(self):
        way = self.way
        self.a = flip(self.sum(0, 4).astype(BF), way.y)
        self.b = flip(self.sum(8, 4).astype(BF), way.x)

    def next(self):
        way, n = self.way, self.n
        a, b = self.a.astype(F32), self.b.astype(F32)
        a_sent = flip((self.sum(4, 2) + a[2 * n :]).astype(BF), way.x)
        b_sent = flip((self.sum(12, 2) + b[2 * n :]).astype(BF), way.y)
        self.a = self.sum(6, 2) + a[: 2 * n] + a_sent.astype(F32)
        self.b = self.sum(14, 2) + b[: 2 * n] + b_sent.astype(F32)

    def low(self):
        self.total = self.a + flip(self.b.astype(BF), self.way.low).astype(F32)

    def high(self):
        total = self.total
        for way in [self.way.high] + self.way.rest:
            half = total.shape[0] // 2
            total = total[:half] + flip(total[half:].astype(BF), way).astype(F32)
        self.total = total[0]


def shards(inputs, items, routes, slots, cotangent, params, momentum, average):
    fsdp, dp = lax.axis_size(FSDP), lax.axis_size(DP)
    devices = fsdp * dp
    share = params.shape[1]
    rows = share // LANES
    padded = -(-(rows + 1) // 16) * 16
    step_rate = RATE_BASE / math.sqrt(CELLS * devices)
    way = ways()
    me = (lax.axis_index(DP) * fsdp + lax.axis_index(FSDP)).astype(jnp.int32).reshape(1)

    gathers = []
    for b in range(BLOCKS):
        own = params[b].astype(BF).reshape(1, rows, LANES)
        gathers.append(Gather(jnp.pad(own, ((0, 0), (0, padded - rows), (0, 0))), way))
    masks, places = [], []
    for b in range(BLOCKS):
        masks.append(window_masks(items.reshape(CELLS), b % 2 == 1))
        places.append(slot_places(routes[b].reshape(CELLS), slots[b].reshape(CELLS)))

    first, second = gathers
    first.far()
    second.own = tie(second.own, first.over)
    first.near()
    second.far()
    first.last()
    hidden = inputs.reshape(CELLS, D)
    saves = []

    w = unpack_weights(me, first.parts, first.runs, rows, devices)
    second.pair, second.over = tie((second.pair, second.over), first.parts)
    second.near()
    h_one, *kept_attn = attn_fwd(False, hidden, w.vec, w.w_in, w.w_out, w.bias, masks[0], (second.over,))
    second.a, second.b = tie((second.a, second.b), h_one)
    second.last()
    following, *kept_moe = moe_fwd(
        h_one, w.vec, w.w1, w.w2, w.b1, w.router, w.router_bias, places[0], F32
    )
    saves.append((hidden, h_one, w, kept_attn, kept_moe))
    hidden = following
    w = unpack_weights(me, second.parts, second.runs, rows, devices, (hidden,))
    h_one, *kept_attn = attn_fwd(True, hidden, w.vec, w.w_in, w.w_out, w.bias, masks[1])
    outputs, *kept_moe = moe_fwd(
        h_one, w.vec, w.w1, w.w2, w.b1, w.router, w.router_bias, places[1], BF
    )
    saves.append((hidden, h_one, w, kept_attn, kept_moe))

    gradient = cotangent.reshape(CELLS, D)
    runs = scatter_runs(way)
    scatters, vectors = [None] * BLOCKS, [None] * BLOCKS
    for b in range(BLOCKS - 1, -1, -1):
        hidden, h_one, w, kept_attn, kept_moe = saves[b]
        shifted = b % 2 == 1
        before = scatters[-1]
        g_one, dw1, dw2, db1, drouter, small_moe = moe_bwd(gradient, h_one, w.vec, w.w1, w.w2, places[b], kept_moe)
        if before is not None:
            before.got = tie(before.got, g_one)
            before.near()
        g_qkv, dw_out, dbias, small_attn = attn_bwd(shifted, g_one, w.w_out, kept_attn[1:])
        if before is not None:
            before.a, before.b = tie((before.a, before.b), g_qkv)
            before.next()
        gradient, dw_in, small_proj = proj_bwd(shifted, g_one, hidden, w.vec, w.w_in, kept_attn[0], g_qkv)
        small = (small_moe, small_attn, small_proj, drouter, db1, dbias)
        keep, send, vectors[b] = pack_grads(me, small, dw_in, dw_out, dw1, dw2, runs, rows, devices, padded)
        if before is not None:
            before.a, before.b = tie((before.a, before.b), send)
        else:
            gradient = tie(gradient, send)
        scatters[b] = Scatter(keep, send, way)
    early, late = scatters[1], scatters[0]
    vector_grads = jnp.stack(vectors)[:, :9]
    vector_grads = vector_grads + flip(vector_grads, way.core)
    early.low()
    late.near()
    early.total, vector_grads = tie((early.total, vector_grads), late.got)
    vector_grads = vector_grads + flip(vector_grads, way.x)
    early.high()
    late.next()
    vector_grads = tie(vector_grads, (late.a, late.b))
    vector_grads = vector_grads + flip(vector_grads, way.y)
    late.low()
    vector_grads = tie(vector_grads, late.total)
    vector_grads = vector_grads + flip(vector_grads, way.low)
    late.high()
    for step in [way.high] + way.rest:
        vector_grads = vector_grads + flip(vector_grads, step)
    grad_all = jnp.stack([scatter.total.reshape(-1)[LAG : LAG + share] for scatter in scatters])
    new_momentum = MOMENTUM_DECAY * momentum + grad_all
    new_params = params - step_rate * (grad_all + MOMENTUM_DECAY * new_momentum)
    new_average = AVERAGE_DECAY * average + (1.0 - AVERAGE_DECAY) * new_params
    return (
        outputs.reshape(1, CELLS, D),
        gradient.reshape(1, CELLS, D),
        new_params,
        new_momentum,
        new_average,
        vector_grads,
    )


def solution(mesh):
    both = (DP, FSDP)
    canvas, vector = P(both), P(None, both)
    return jax.shard_map(
        shards,
        mesh=mesh,
        in_specs=(canvas, canvas, vector, vector, canvas, vector, vector, vector),
        out_specs=(canvas, canvas, vector, vector, vector, P()),
        check_vma=False,
    )
```

time: 516 us -> 346 us (0.67); the launches traced: 507 us -> 343 us
  Pallas kernels: 204 us -> 149 us
  waiting for transfers between devices: 184 us -> 130 us
  local copies, waits for them, and re-layouts: 42.6 us -> 10.5 us
  other arithmetic: 30 us -> 8.49 us
  between operations: 16.6 us -> 1.63 us
  starting transfers between devices: 26.3 us -> 41.1 us
    all_gather x2 -> x0, waiting for transfers between devices: 129 us -> none  [shards(): gathered.append(lax.all_gather(own, (DP, FSDP), axis=0, tiled=True))]
    ppermute x25 -> x39, waiting for transfers between devices: 54.8 us -> 130 us  [flip(): lax.ppermute(array, axis, [(i, i ^ 1 << bit) for i in range(lax.axis_size...]
    pallas_call x12 -> x20, Pallas kernels: 204 us -> 149 us  [call(): return lambda *args: run(*args, *deps)]
    ppermute x25 -> x39, starting transfers between devices: 26.3 us -> 41.1 us  [flip(): lax.ppermute(array, axis, [(i, i ^ 1 << bit) for i in range(lax.axis_size...]
    slice x29 -> x7, local copies, waits for them, and re-layouts: 13.2 us -> 2.33 us  [the longest x1 1.95 us: shards(): own = params[b].astype(BF).reshape(1, rows, LANES)]
    dynamic_slice x4 -> x0, local copies, waits for them, and re-layouts: 9.32 us -> none  [halve(): send = lax.dynamic_slice_in_dim(keep, (1 - mine) * half, half).astype(BF)]
    add x25 -> x12, other arithmetic: 9.15 us -> 0.86 us  [the longest x2 0.35 us: next(): self.b = self.sum(14, 2) + b[:2 * n] + b_sent.astype(F32)]
    convert_element_type x9 -> x8, other arithmetic: 8.45 us -> 1.68 us  [the longest x4 0.4 us: next(): a, b = (self.a.astype(F32), self.b.astype(F32))]
  transfers between devices with their start and end apart: 27 -> 39, of which waited for: 18 -> 24; matrix products, arithmetic and copies ran while one was open for 8% -> 2% of each run, Pallas kernels for 4% -> 11%
where the time goes in v1:
time: 346 us; the launch traced here: 343 us
  Pallas kernels  149 us (43%)
  waiting for transfers between devices  130 us (38%)
  starting transfers between devices  41.1 us (12%)
  local copies, waits for them, and re-layouts  10.5 us (3%)
  other arithmetic  8.49 us (2%)
    pallas_call x20, Pallas kernels, call(): return lambda *args: run(*args, *deps)  149 us
    ppermute x39, waiting for transfers between devices, flip(): lax.ppermute(array, axis, [(i, i ^ 1 << bit) for i in range(lax.axis_size...  130 us
    ppermute x39, starting transfers between devices, flip(): lax.ppermute(array, axis, [(i, i ^ 1 << bit) for i in range(lax.axis_size...  41.1 us
    unnamed x67, local copies, waits for them, and re-layouts  7.2 us
  transfers between devices with their start and end apart: 39, of which 24 were waited for; matrix products, arithmetic and copies ran while one was open for 2% of the time, Pallas kernels for 11%

profile of v1, /device:TPU:0, one launch (start us, length us, event | category | flops | bytes accessed | tf_op | source)
XLA Modules:
  0.0 342.9 jit_solution(975187215013061712)
XLA Ops:
  4.0 4.1 %collective-permute-start = (bf16[1,736,128]{2,1,0:T(8,128)(2,1)S(1)}, bf16[1,736,128]{2,1,0:T(8,128)(2,1)S(1)}, u32[]{:S(2)}, u32[]{:S(2)}) collective-permute-start(bf16[1,736,128]{2,1,0:T(8,128)(2,1)S(1)} %pad.7.refs_0_), channel_id=1, source_target_pairs={{0,16},{4,20},{8,24},{12,28},{16,0},{20,4},{24,8},{28,12},{1,17},{... | collective-permute-start | bytes 565256 | tf_op jit(solution)/shard_map/ppermute | solution.py:769
  8.1 8.8 %collective-permute-done.refs_1_ = bf16[1,736,128]{2,1,0:T(8,128)(2,1)S(1)} collective-permute-done((bf16[1,736,128]{2,1,0:T(8,128)(2,1)S(1)}, bf16[1,736,128]{2,1,0:T(8,128)(2,1)S(1)}, u32[]{:S(2)}, u32[]{:S(2)}) %collective-permute-start) | collective-permute-done | bytes 188448 | tf_op jit(solution)/shard_map/ppermute | solution.py:769
  19.2 7.7 %collective-permute-done.3.refs_0_ = bf16[2,736,128]{2,1,0:T(8,128)(2,1)S(1)} collective-permute-done((bf16[2,736,128]{2,1,0:T(8,128)(2,1)S(1)}, bf16[2,736,128]{2,1,0:T(8,128)(2,1)S(1)}, u32[]{:S(2)}, u32[]{:S(2)}) %collective-permute-start.3) | collective-permute-done | bytes 376864 | tf_op jit(solution)/shard_map/ppermute | solution.py:769
  30.2 8.3 %collective-permute-done.4.refs_1_ = bf16[2,736,128]{2,1,0:T(8,128)(2,1)S(1)} collective-permute-done((bf16[2,736,128]{2,1,0:T(8,128)(2,1)S(1)}, bf16[2,736,128]{2,1,0:T(8,128)(2,1)S(1)}, u32[]{:S(2)}, u32[]{:S(2)}) %collective-permute-start.4) | collective-permute-done | bytes 376864 | tf_op jit(solution)/shard_map/ppermute | solution.py:769
  41.6 3.4 collective-permute-start.10
  45.1 6.9 %collective-permute-done.2.refs_2_ = bf16[4,736,128]{2,1,0:T(8,128)(2,1)S(1)} collective-permute-done((bf16[4,736,128]{2,1,0:T(8,128)(2,1)S(1)}, bf16[4,736,128]{2,1,0:T(8,128)(2,1)S(1)}, u32[]{:S(2)}, u32[]{:S(2)}) %collective-permute-start.2) | collective-permute-done | bytes 753696 | tf_op jit(solution)/shard_map/ppermute | solution.py:769
  56.1 9.2 %collective-permute-done.11.refs_6_.refs_0_ = bf16[2,736,128]{2,1,0:T(8,128)(2,1)} collective-permute-done((bf16[2,736,128]{2,1,0:T(8,128)(2,1)S(1)}, bf16[2,736,128]{2,1,0:T(8,128)(2,1)}, u32[]{:S(2)}, u32[]{:S(2)}) %collective-permute-start.11) | collective-permute-done | bytes 376864 | tf_op jit(solution)/shard_map/ppermute | solution.py:769
  68.4 11.2 %shard_map.139 = (bf16[384,1152]{1,0:T(8,128)(2,1)S(1)}, bf16[384,384]{1,0:T(8,128)(2,1)S(1)}, bf16[768,1536]{1,0:T(8,128)(2,1)S(1)}, bf16[3072,384]{1,0:T(8,128...) custom-call(s32[1]{0:T(128)} %bitcast.1.refs_0_, ...), custom_call_target="tpu_custom_call" | custom-call | flops 11000000512 | tf_op jit(solution)/shard_map/pallas_call | solution.py:62
  79.6 16.8 %shard_map.141 = (f32[784,384]{1,0:T(8,128)S(1)}, bf16[1024,384]{1,0:T(8,128)(2,1)S(1)}, bf16[1024,1152]{1,0:T(8,128)(2,1)S(1)}, bf16[1024,384]{1,0:T(8,128)(2,1)S(1)}, bf16[48,64,256]{2,1,0:T(8,128)(2,1)S(1)}) custom-call(bf16[784,384]{1,0:T(8,128)(2,1)S(1)} %bitcast.28, f32[16,384]{1,0:T(8,128)S(1)} %get-tuple-element.95.refs_1_.refs_2_, ...), custom_call_target="tpu_custom_call" | custom-call | flops 18699999232 | tf_op jit(solution)/shard_map/pallas_call | solution.py:62
  100.9 15.9 %collective-permute-done.14.refs_2_ = bf16[4,736,128]{2,1,0:T(8,128)(2,1)S(1)} collective-permute-done((bf16[4,736,128]{2,1,0:T(8,128)(2,1)S(1)}, bf16[4,736,128]{2,1,0:T(8,128)(2,1)S(1)}, u32[]{:S(2)}, u32[]{:S(2)}) %collective-permute-start.14) | collective-permute-done | bytes 753696 | tf_op jit(solution)/shard_map/ppermute | solution.py:769
  117.5 9.1 %shard_map.142 = (f32[784,384]{1,0:T(8,128)S(1)}, bf16[784,384]{1,0:T(8,128)(2,1)S(1)}, bf16[1024,384]{1,0:T(8,128)(2,1)S(1)}, bf16[1024,1536]{1,0:T(8,128)(2,1)...) custom-call(f32[784,384]{1,0:T(8,128)S(1)} %get-tuple-element.101.refs_0_.refs_1_, ...), custom_call_target="tpu_custom_call" | custom-call | flops 10449999872 | tf_op jit(solution)/shard_map/pallas_call | solution.py:62
  127.3 9.3 %shard_map.145 = (bf16[384,1152]{1,0:T(8,128)(2,1)S(1)}, bf16[384,384]{1,0:T(8,128)(2,1)S(1)}, bf16[768,1536]{1,0:T(8,128)(2,1)S(1)}, bf16[3072,384]{1,0:T(8,128...) custom-call(s32[1]{0:T(128)} %bitcast.1.refs_0_, ...), custom_call_target="tpu_custom_call" | custom-call | flops 11000000512 | tf_op jit(solution)/shard_map/pallas_call | solution.py:62
  136.7 17.0 %shard_map.146 = (f32[784,384]{1,0:T(8,128)S(1)}, bf16[1024,384]{1,0:T(8,128)(2,1)S(1)}, bf16[1024,1152]{1,0:T(8,128)(2,1)S(1)}, bf16[1024,384]{1,0:T(8,128)(2,1)S(1)}, bf16[48,64,256]{2,1,0:T(8,128)(2,1)S(1)}) custom-call(f32[784,384]{1,0:T(8,128)S(1)} %get-tuple-element.107.refs_9_.refs_0_.refs_1_, f32[16,384]{1,0:T(8,128)S(1)} %get-tuple-element.111.refs_1_.refs_2_, ...), custom_call_target="tpu_custom_call" | custom-call | flops 18699999232 | tf_op jit(solution)/shard_map/pallas_call | solution.py:62
  155.3 9.8 %shard_map.147 = (bf16[784,384]{1,0:T(8,128)(2,1)}, bf16[784,384]{1,0:T(8,128)(2,1)S(1)}, bf16[1024,384]{1,0:T(8,128)(2,1)S(1)}, bf16[1024,1536]{1,0:T(8,128)(2,...) custom-call(f32[784,384]{1,0:T(8,128)S(1)} %get-tuple-element.115.refs_0_.refs_1_, ...), custom_call_target="tpu_custom_call" | custom-call | flops 10449999872 | tf_op jit(solution)/shard_map/pallas_call | solution.py:62
  165.1 10.4 %shard_map.148 = (f32[784,384]{1,0:T(8,128)S(1)}, f32[2,384,1536]{2,1,0:T(8,128)S(1)}, f32[2,1536,384]{2,1,0:T(8,128)S(1)}, f32[8,1536]{1,0:T(8,128)S(1)}, f32[8,384]{1,0:T(8,128)S(1)}, /*index=5*/f32[16,384]{1,0:T(8,128)S(1)}) custom-call(bf16[784,384]{1,0:T(8,128)(2,1)S(1)} %bitcast.27, f32[784,384]{1,0:T(8,128)S(1)} %get-tuple-element.115.refs_0_.refs_1_, ...), custom_call_target="tpu_custom_call" | custom-call | flops 11550000128 | tf_op jit(solution)/shard_map/pallas_call | solution.py:62
  177.2 16.7 %shard_map.149 = (bf16[1024,1152]{1,0:T(8,128)(2,1)S(1)}, f32[384,384]{1,0:T(8,128)S(1)}, f32[3,64,256]{2,1,0:T(8,128)S(1)}, f32[16,384]{1,0:T(8,128)S(1)}) custom-call(f32[784,384]{1,0:T(8,128)S(1)} %get-tuple-element.128.refs_0_, bf16[384,384]{1,0:T(8,128)(2,1)S(1)} %get-tuple-element.113.refs_3_.refs_1_, bf16[1024,1152]{1,0:T(8,128)(2,1)S(1)} %copy-done.17, ...), custom_call_target="tpu_custom_call" | custom-call | flops 18150000640 | tf_op jit(solution)/shard_map/pallas_call | solution.py:62
  193.9 5.2 %shard_map.150 = (f32[784,384]{1,0:T(8,128)S(1)}, f32[384,1152]{1,0:T(8,128)S(1)}, f32[16,384]{1,0:T(8,128)S(1)}) custom-call(f32[784,384]{1,0:T(8,128)S(1)} %get-tuple-element.128.refs_0_, f32[784,384]{1,0:T(8,128)S(1)} %get-tuple-element.107.refs_9_.refs_0_.refs_1_, f32[16,384]{1,0:T(8,128)S(1)} %get-tuple-element.111.refs_1_.refs_2_, ...), custom_call_target="tpu_custom_call" | custom-call | flops 6049999872 | tf_op jit(solution)/shard_map/pallas_call | solution.py:62
  199.2 4.1 %shard_map.151 = (bf16[16,736,128]{2,1,0:T(8,128)(2,1)S(1)}, bf16[16,736,128]{2,1,0:T(8,128)(2,1)S(1)}, f32[16,384]{1,0:T(8,128)S(1)}) custom-call(s32[1]{0:T(128)} %bitcast.1.refs_0_, f32[16,384]{1,0:T(8,128)S(1)} %get-tuple-element.135.refs_1_, f32[16,384]{1,0:T(8,128)S(1)} %get-tuple-element.136.refs_2_, f32[16,384]{1,0:T(8,128)S(1)} %get-tuple-element.137.refs_3_, ...), custom_call_target="tpu_custom_call" | custom-call | flops 4400000000 | tf_op jit(solution)/shard_map/pallas_call | solution.py:62
  205.2 10.7 %shard_map.152 = (f32[784,384]{1,0:T(8,128)S(1)}, f32[2,384,1536]{2,1,0:T(8,128)S(1)}, f32[2,1536,384]{2,1,0:T(8,128)S(1)}, f32[8,1536]{1,0:T(8,128)S(1)}, f32[8,384]{1,0:T(8,128)S(1)}, /*index=5*/f32[16,384]{1,0:T(8,128)S(1)}) custom-call(f32[784,384]{1,0:T(8,128)S(1)} %get-tuple-element.146.refs_0_, f32[784,384]{1,0:T(8,128)S(1)} %copy-done.9, ...), custom_call_target="tpu_custom_call" | custom-call | flops 11550000128 | tf_op jit(solution)/shard_map/pallas_call | solution.py:62
  216.0 16.6 %shard_map.153 = (bf16[1024,1152]{1,0:T(8,128)(2,1)S(1)}, f32[384,384]{1,0:T(8,128)S(1)}, f32[3,64,256]{2,1,0:T(8,128)S(1)}, f32[16,384]{1,0:T(8,128)S(1)}) custom-call(f32[784,384]{1,0:T(8,128)S(1)} %get-tuple-element.153.refs_0_, bf16[384,384]{1,0:T(8,128)(2,1)S(1)} %copy-done.23, bf16[1024,1152]{1,0:T(8,128)(2,1)S(1)} %copy-done.15, ...), custom_call_target="tpu_custom_call" | custom-call | flops 18150000640 | tf_op jit(solution)/shard_map/pallas_call | solution.py:62
  232.6 6.3 %shard_map.154 = (f32[784,384]{1,0:T(8,128)}, f32[384,1152]{1,0:T(8,128)S(1)}, f32[16,384]{1,0:T(8,128)S(1)}) custom-call(f32[784,384]{1,0:T(8,128)S(1)} %get-tuple-element.153.refs_0_, bf16[784,384]{1,0:T(8,128)(2,1)S(1)} %bitcast.29, f32[16,384]{1,0:T(8,128)S(1)} %get-tuple-element.95.refs_1_.refs_2_, bf16[384,1152]{1,0:T(8,128)(2,1)S(1)} %copy-done.7, ...), custom_call_target="tpu_custom_call" | custom-call | flops 6049999872 | tf_op jit(solution)/shard_map/pallas_call | solution.py:62
  238.9 4.3 %shard_map.155 = (bf16[16,736,128]{2,1,0:T(8,128)(2,1)S(1)}, bf16[16,736,128]{2,1,0:T(8,128)(2,1)S(1)}, f32[16,384]{1,0:T(8,128)S(1)}) custom-call(s32[1]{0:T(128)} %bitcast.1.refs_0_, f32[16,384]{1,0:T(8,128)S(1)} %get-tuple-element.160.refs_1_, f32[16,384]{1,0:T(8,128)S(1)} %get-tuple-element.161.refs_2_, f32[16,384]{1,0:T(8,128)S(1)} %get-tuple-element.162.refs_3_, ...), custom_call_target="tpu_custom_call" | custom-call | flops 4400000000 | tf_op jit(solution)/shard_map/pallas_call | solution.py:62
  243.7 5.0 %collective-permute-done.20 = bf16[16,736,128]{2,1,0:T(8,128)(2,1)S(1)} collective-permute-done((bf16[16,736,128]{2,1,0:T(8,128)(2,1)S(1)}, bf16[16,736,128]{2,1,0:T(8,128)(2,1)S(1)}, u32[]{:S(2)}, u32[]{:S(2)}) %collective-permute-start.20) | collective-permute-done | bytes 3014688 | tf_op jit(solution)/shard_map/ppermute | solution.py:769
  255.2 13.6 %collective-permute-done.21 = bf16[4,736,128]{2,1,0:T(8,128)(2,1)S(1)} collective-permute-done((bf16[4,736,128]{2,1,0:T(8,128)(2,1)S(1)}, bf16[4,736,128]{2,1,0:T(8,128)(2,1)S(1)}, u32[]{:S(2)}, u32[]{:S(2)}) %collective-permute-start.21) | collective-permute-done | bytes 753696 | tf_op jit(solution)/shard_map/ppermute | solution.py:769
  271.3 14.2 %collective-permute-done.29 = bf16[4,736,128]{2,1,0:T(8,128)(2,1)S(1)} collective-permute-done((bf16[4,736,128]{2,1,0:T(8,128)(2,1)S(1)}, bf16[4,736,128]{2,1,0:T(8,128)(2,1)S(1)}, u32[]{:S(2)}, u32[]{:S(2)}) %collective-permute-start.29) | collective-permute-done | bytes 753696 | tf_op jit(solution)/shard_map/ppermute | solution.py:769
  289.0 4.1 %collective-permute-done.24 = bf16[2,736,128]{2,1,0:T(8,128)(2,1)S(1)} collective-permute-done((bf16[2,736,128]{2,1,0:T(8,128)(2,1)S(1)}, bf16[2,736,128]{2,1,0:T(8,128)(2,1)S(1)}, u32[]{:S(2)}, u32[]{:S(2)}) %collective-permute-start.24) | collective-permute-done | bytes 376864 | tf_op jit(solution)/shard_map/ppermute | solution.py:769
  304.3 3.9 %collective-permute-start.26 = (bf16[1,736,128]{2,1,0:T(8,128)(2,1)S(1)}, bf16[1,736,128]{2,1,0:T(8,128)(2,1)S(1)}, u32[]{:S(2)}, u32[]{:S(2)}) collective-permute-start(bf16[1,736,128]{2,1,0:T(8,128)(2,1)S(1)} %slice.278), channel_id=1, source_target_pairs={{0,16},{4,20},{8,24},{12,28},{16,0},{20,4},{24,8},{28,12},{1,17},{... | collective-permute-start | bytes 565256 | tf_op jit(solution)/shard_map/ppermute | solution.py:769
  308.1 6.6 %collective-permute-done.32 = bf16[2,736,128]{2,1,0:T(8,128)(2,1)S(1)} collective-permute-done((bf16[2,736,128]{2,1,0:T(8,128)(2,1)S(1)}, bf16[2,736,128]{2,1,0:T(8,128)(2,1)S(1)}, u32[]{:S(2)}, u32[]{:S(2)}) %collective-permute-start.32) | collective-permute-done | bytes 376864 | tf_op jit(solution)/shard_map/ppermute | solution.py:769
  315.3 3.7 %collective-permute-done.35 = f32[2,9,384]{2,1,0:T(8,128)S(1)} collective-permute-done((f32[2,9,384]{2,1,0:T(8,128)S(1)}, f32[2,9,384]{2,1,0:T(8,128)S(1)}, u32[]{:S(2)}, u32[]{:S(2)}) %collective-permute-start.35) | collective-permute-done | bytes 27680 | tf_op jit(solution)/shard_map/ppermute | solution.py:769
  323.3 4.3 %collective-permute-done.37 = f32[2,9,384]{2,1,0:T(8,128)S(1)} collective-permute-done((f32[2,9,384]{2,1,0:T(8,128)S(1)}, f32[2,9,384]{2,1,0:T(8,128)S(1)}, u32[]{:S(2)}, u32[]{:S(2)}) %collective-permute-start.37) | collective-permute-done | bytes 27680 | tf_op jit(solution)/shard_map/ppermute | solution.py:769
  334.5 4.3 %collective-permute-done.34 = bf16[1,736,128]{2,1,0:T(8,128)(2,1)S(1)} collective-permute-done((bf16[1,736,128]{2,1,0:T(8,128)(2,1)S(1)}, bf16[1,736,128]{2,1,0:T(8,128)(2,1)S(1)}, u32[]{:S(2)}, u32[]{:S(2)}) %collective-permute-start.34) | collective-permute-done | bytes 188448 | tf_op jit(solution)/shard_map/ppermute | solution.py:769
  339.4 3.3 multiply_add_fusion
  (187 shorter events, 66.3 us)
Async XLA Ops:
  4.0 12.9 %collective-permute-start = (bf16[1,736,128]{2,1,0:T(8,128)(2,1)S(1)}, bf16[1,736,128]{2,1,0:T(8,128)(2,1)S(1)}, u32[]{:S(2)}, u32[]{:S(2)}) collective-permute-start(bf16[1,736,128]{2,1,0:T(8,128)(2,1)S(1)} %pad.7.refs_0_), channel_id=1, source_target_pairs={{0,16},{4,20},{8,24},{12,28},{16,0},{20,4},{24,8},{28,12},{1,17},{... | collective-permute-start | bytes 565256 | tf_op jit(solution)/shard_map/ppermute | solution.py:769
  16.9 10.0 %collective-permute-start.3 = (bf16[2,736,128]{2,1,0:T(8,128)(2,1)S(1)}, bf16[2,736,128]{2,1,0:T(8,128)(2,1)S(1)}, u32[]{:S(2)}, u32[]{:S(2)}) collective-permute-start(bf16[2,736,128]{2,1,0:T(8,128)(2,1)S(1)} %shard_map.136.refs_0_), channel_id=1, source_target_pairs={{0,8},{4,12},{8,0},{12,4},{16,24},{20,28},{24,16},{28,20},{1,9},{5... | collective-permute-start | bytes 1130504 | tf_op jit(solution)/shard_map/ppermute | solution.py:769
  17.7 10.5 %collective-permute-start.1 = (bf16[2,736,128]{2,1,0:T(8,128)(2,1)S(1)}, bf16[2,736,128]{2,1,0:T(8,128)(2,1)S(1)}, u32[]{:S(2)}, u32[]{:S(2)}) collective-permute-start(bf16[2,736,128]{2,1,0:T(8,128)(2,1)S(1)} %shard_map.136.refs_0_), channel_id=1, source_target_pairs={{0,2},{1,3},{2,0},{3,1},{4,6},{5,7},{6,4},{7,5},{8,10},{9,11},{10,... | collective-permute-start | bytes 1130504 | tf_op jit(solution)/shard_map/ppermute | solution.py:769
  26.9 11.7 %collective-permute-start.4 = (bf16[2,736,128]{2,1,0:T(8,128)(2,1)S(1)}, bf16[2,736,128]{2,1,0:T(8,128)(2,1)S(1)}, u32[]{:S(2)}, u32[]{:S(2)}) collective-permute-start(bf16[2,736,128]{2,1,0:T(8,128)(2,1)S(1)} %collective-permute-done.3.refs_0_), channel_id=1, source_target_pairs={{0,4},{4,0},{8,12},{12,8},{16,20},{20,16},{24,28},{28,24},{1,5},{5... | collective-permute-start | bytes 1130504 | tf_op jit(solution)/shard_map/ppermute | solution.py:769
  28.8 23.3 %collective-permute-start.2 = (bf16[4,736,128]{2,1,0:T(8,128)(2,1)S(1)}, bf16[4,736,128]{2,1,0:T(8,128)(2,1)S(1)}, u32[]{:S(2)}, u32[]{:S(2)}) collective-permute-start(bf16[4,736,128]{2,1,0:T(8,128)(2,1)S(1)} %shard_map.137.refs_1_), channel_id=1, source_target_pairs={{0,4},{4,0},{8,12},{12,8},{16,20},{20,16},{24,28},{28,24},{1,5},{5... | collective-permute-start | bytes 2261000 | tf_op jit(solution)/shard_map/ppermute | solution.py:769
  38.7 13.6 %collective-permute-start.5 = (bf16[4,736,128]{2,1,0:T(8,128)(2,1)S(1)}, bf16[4,736,128]{2,1,0:T(8,128)(2,1)S(1)}, u32[]{:S(2)}, u32[]{:S(2)}) collective-permute-start(bf16[4,736,128]{2,1,0:T(8,128)(2,1)S(1)} %shard_map.138.refs_3_), channel_id=1, source_target_pairs={{0,2},{1,3},{2,0},{3,1},{4,6},{5,7},{6,4},{7,5},{8,10},{9,11},{10,... | collective-permute-start | bytes 2261000 | tf_op jit(solution)/shard_map/ppermute | solution.py:769
  41.5 23.8 %collective-permute-start.6 = (bf16[4,736,128]{2,1,0:T(8,128)(2,1)S(1)}, bf16[4,736,128]{2,1,0:T(8,128)(2,1)}, u32[]{:S(2)}, u32[]{:S(2)}) collective-permute-start(bf16[4,736,128]{2,1,0:T(8,128)(2,1)S(1)} %shard_map.137.refs_1_), channel_id=1, source_target_pairs={{0,1},{1,0},{2,3},{3,2},{4,5},{5,4},{6,7},{7,6},{8,9},{9,8},{10,11... | collective-permute-start | bytes 2261000 | tf_op jit(solution)/shard_map/ppermute | solution.py:769
  41.6 12.8 %collective-permute-start.10 = (bf16[1,736,128]{2,1,0:T(8,128)(2,1)S(1)}, bf16[1,736,128]{2,1,0:T(8,128)(2,1)S(1)}, u32[]{:S(2)}, u32[]{:S(2)}) collective-permute-start(bf16[1,736,128]{2,1,0:T(8,128)(2,1)S(1)} %pad.8.refs_0_), channel_id=1, source_target_pairs={{0,16},{4,20},{8,24},{12,28},{16,0},{20,4},{24,8},{28,12},{1,17},{... | collective-permute-start | bytes 565256 | tf_op jit(solution)/shard_map/ppermute | solution.py:769
  45.0 20.3 %collective-permute-start.8 = (bf16[4,736,128]{2,1,0:T(8,128)(2,1)S(1)}, bf16[4,736,128]{2,1,0:T(8,128)(2,1)}, u32[]{:S(2)}, u32[]{:S(2)}) collective-permute-start(bf16[4,736,128]{2,1,0:T(8,128)(2,1)S(1)} %shard_map.138.refs_3_), channel_id=1, source_target_pairs={{0,1},{1,0},{2,3},{3,2},{4,5},{5,4},{6,7},{7,6},{8,9},{9,8},{10,11... | collective-permute-start | bytes 2261000 | tf_op jit(solution)/shard_map/ppermute | solution.py:769
  52.1 13.2 %collective-permute-start.7 = (bf16[4,736,128]{2,1,0:T(8,128)(2,1)S(1)}, bf16[4,736,128]{2,1,0:T(8,128)(2,1)}, u32[]{:S(2)}, u32[]{:S(2)}) collective-permute-start(bf16[4,736,128]{2,1,0:T(8,128)(2,1)S(1)} %collective-permute-done.2.refs_2_), channel_id=1, source_target_pairs={{0,1},{1,0},{2,3},{3,2},{4,5},{5,4},{6,7},{7,6},{8,9},{9,8},{10,11... | collective-permute-start | bytes 2261000 | tf_op jit(solution)/shard_map/ppermute | solution.py:769
  52.2 13.1 %collective-permute-start.9 = (bf16[4,736,128]{2,1,0:T(8,128)(2,1)S(1)}, bf16[4,736,128]{2,1,0:T(8,128)(2,1)}, u32[]{:S(2)}, u32[]{:S(2)}) collective-permute-start(bf16[4,736,128]{2,1,0:T(8,128)(2,1)S(1)} %collective-permute-done.5.refs_4_), channel_id=1, source_target_pairs={{0,1},{1,0},{2,3},{3,2},{4,5},{5,4},{6,7},{7,6},{8,9},{9,8},{10,11... | collective-permute-start | bytes 2261000 | tf_op jit(solution)/shard_map/ppermute | solution.py:769
  54.4 11.0 %collective-permute-start.11 = (bf16[2,736,128]{2,1,0:T(8,128)(2,1)S(1)}, bf16[2,736,128]{2,1,0:T(8,128)(2,1)}, u32[]{:S(2)}, u32[]{:S(2)}) collective-permute-start(bf16[2,736,128]{2,1,0:T(8,128)(2,1)S(1)} %shard_map.140.refs_0_), channel_id=1, source_target_pairs={{0,8},{4,12},{8,0},{12,4},{16,24},{20,28},{24,16},{28,20},{1,9},{5... | collective-permute-start | bytes 1130504 | tf_op jit(solution)/shard_map/ppermute | solution.py:769
  65.3 31.2 %collective-permute-start.12 = (bf16[2,736,128]{2,1,0:T(8,128)(2,1)S(1)}, bf16[2,736,128]{2,1,0:T(8,128)(2,1)S(1)}, u32[]{:S(2)}, u32[]{:S(2)}) collective-permute-start(bf16[2,736,128]{2,1,0:T(8,128)(2,1)S(1)} %shard_map.140.refs_0_), channel_id=1, source_target_pairs={{0,2},{1,3},{2,0},{3,1},{4,6},{5,7},{6,4},{7,5},{8,10},{9,11},{10,... | collective-permute-start | bytes 1130504 | tf_op jit(solution)/shard_map/ppermute | solution.py:769
  66.9 29.7 %collective-permute-start.13 = (bf16[2,736,128]{2,1,0:T(8,128)(2,1)}, bf16[2,736,128]{2,1,0:T(8,128)(2,1)S(1)}, u32[]{:S(2)}, u32[]{:S(2)}) collective-permute-start(bf16[2,736,128]{2,1,0:T(8,128)(2,1)} %collective-permute-done.11.refs_6_.refs_0_), channel_id=1, source_target_pairs={{0,4},{4,0},{8,12},{12,8},{16,20},{20,16},{24,28},{28,24},{1,5},{5... | collective-permute-start | bytes 1130504 | tf_op jit(solution)/shard_map/ppermute | solution.py:769
  98.7 18.1 %collective-permute-start.14 = (bf16[4,736,128]{2,1,0:T(8,128)(2,1)S(1)}, bf16[4,736,128]{2,1,0:T(8,128)(2,1)S(1)}, u32[]{:S(2)}, u32[]{:S(2)}) collective-permute-start(bf16[4,736,128]{2,1,0:T(8,128)(2,1)S(1)} %shard_map.143.refs_1_), channel_id=1, source_target_pairs={{0,4},{4,0},{8,12},{12,8},{16,20},{20,16},{24,28},{28,24},{1,5},{5... | collective-permute-start | bytes 2261000 | tf_op jit(solution)/shard_map/ppermute | solution.py:769
  99.2 17.8 %collective-permute-start.15 = (bf16[4,736,128]{2,1,0:T(8,128)(2,1)S(1)}, bf16[4,736,128]{2,1,0:T(8,128)(2,1)S(1)}, u32[]{:S(2)}, u32[]{:S(2)}) collective-permute-start(bf16[4,736,128]{2,1,0:T(8,128)(2,1)S(1)} %shard_map.144.refs_3_), channel_id=1, source_target_pairs={{0,2},{1,3},{2,0},{3,1},{4,6},{5,7},{6,4},{7,5},{8,10},{9,11},{10,... | collective-permute-start | bytes 2261000 | tf_op jit(solution)/shard_map/ppermute | solution.py:769
  100.3 27.0 %collective-permute-start.16 = (bf16[4,736,128]{2,1,0:T(8,128)(2,1)S(1)}, bf16[4,736,128]{2,1,0:T(8,128)(2,1)S(1)}, u32[]{:S(2)}, u32[]{:S(2)}) collective-permute-start(bf16[4,736,128]{2,1,0:T(8,128)(2,1)S(1)} %shard_map.143.refs_1_), channel_id=1, source_target_pairs={{0,1},{1,0},{2,3},{3,2},{4,5},{5,4},{6,7},{7,6},{8,9},{9,8},{10,11... | collective-permute-start | bytes 2261000 | tf_op jit(solution)/shard_map/ppermute | solution.py:769
  100.4 26.9 %collective-permute-start.18 = (bf16[4,736,128]{2,1,0:T(8,128)(2,1)S(1)}, bf16[4,736,128]{2,1,0:T(8,128)(2,1)S(1)}, u32[]{:S(2)}, u32[]{:S(2)}) collective-permute-start(bf16[4,736,128]{2,1,0:T(8,128)(2,1)S(1)} %shard_map.144.refs_3_), channel_id=1, source_target_pairs={{0,1},{1,0},{2,3},{3,2},{4,5},{5,4},{6,7},{7,6},{8,9},{9,8},{10,11... | collective-permute-start | bytes 2261000 | tf_op jit(solution)/shard_map/ppermute | solution.py:769
  116.8 10.6 %collective-permute-start.17 = (bf16[4,736,128]{2,1,0:T(8,128)(2,1)S(1)}, bf16[4,736,128]{2,1,0:T(8,128)(2,1)S(1)}, u32[]{:S(2)}, u32[]{:S(2)}) collective-permute-start(bf16[4,736,128]{2,1,0:T(8,128)(2,1)S(1)} %collective-permute-done.14.refs_2_), channel_id=1, source_target_pairs={{0,1},{1,0},{2,3},{3,2},{4,5},{5,4},{6,7},{7,6},{8,9},{9,8},{10,11... | collective-permute-start | bytes 2261000 | tf_op jit(solution)/shard_map/ppermute | solution.py:769
  117.0 10.3 %collective-permute-start.19 = (bf16[4,736,128]{2,1,0:T(8,128)(2,1)S(1)}, bf16[4,736,128]{2,1,0:T(8,128)(2,1)S(1)}, u32[]{:S(2)}, u32[]{:S(2)}) collective-permute-start(bf16[4,736,128]{2,1,0:T(8,128)(2,1)S(1)} %collective-permute-done.15.refs_4_), channel_id=1, source_target_pairs={{0,1},{1,0},{2,3},{3,2},{4,5},{5,4},{6,7},{7,6},{8,9},{9,8},{10,11... | collective-permute-start | bytes 2261000 | tf_op jit(solution)/shard_map/ppermute | solution.py:769
  249.1 19.7 %collective-permute-start.21 = (bf16[4,736,128]{2,1,0:T(8,128)(2,1)S(1)}, bf16[4,736,128]{2,1,0:T(8,128)(2,1)S(1)}, u32[]{:S(2)}, u32[]{:S(2)}) collective-permute-start(bf16[4,736,128]{2,1,0:T(8,128)(2,1)S(1)} %get-tuple-element.205), channel_id=1, source_target_pairs={{0,4},{4,0},{8,12},{12,8},{16,20},{20,16},{24,28},{28,24},{1,5},{5... | collective-permute-start | bytes 2261000 | tf_op jit(solution)/shard_map/ppermute | solution.py:769
  250.5 19.7 %collective-permute-start.23 = (bf16[4,736,128]{2,1,0:T(8,128)(2,1)S(1)}, bf16[4,736,128]{2,1,0:T(8,128)(2,1)S(1)}, u32[]{:S(2)}, u32[]{:S(2)}) collective-permute-start(bf16[4,736,128]{2,1,0:T(8,128)(2,1)S(1)} %get-tuple-element.206), channel_id=1, source_target_pairs={{0,2},{1,3},{2,0},{3,1},{4,6},{5,7},{6,4},{7,5},{8,10},{9,11},{10,... | collective-permute-start | bytes 2261000 | tf_op jit(solution)/shard_map/ppermute | solution.py:769
  253.4 32.1 %collective-permute-start.29 = (bf16[4,736,128]{2,1,0:T(8,128)(2,1)S(1)}, bf16[4,736,128]{2,1,0:T(8,128)(2,1)S(1)}, u32[]{:S(2)}, u32[]{:S(2)}) collective-permute-start(bf16[4,736,128]{2,1,0:T(8,128)(2,1)S(1)} %get-tuple-element.209), channel_id=1, source_target_pairs={{0,2},{1,3},{2,0},{3,1},{4,6},{5,7},{6,4},{7,5},{8,10},{9,11},{10,... | collective-permute-start | bytes 2261000 | tf_op jit(solution)/shard_map/ppermute | solution.py:769
  253.8 31.7 %collective-permute-start.28 = (bf16[4,736,128]{2,1,0:T(8,128)(2,1)S(1)}, bf16[4,736,128]{2,1,0:T(8,128)(2,1)S(1)}, u32[]{:S(2)}, u32[]{:S(2)}) collective-permute-start(bf16[4,736,128]{2,1,0:T(8,128)(2,1)S(1)} %get-tuple-element.210), channel_id=1, source_target_pairs={{0,4},{4,0},{8,12},{12,8},{16,20},{20,16},{24,28},{28,24},{1,5},{5... | collective-permute-start | bytes 2261000 | tf_op jit(solution)/shard_map/ppermute | solution.py:769
  270.6 22.5 %collective-permute-start.24 = (bf16[2,736,128]{2,1,0:T(8,128)(2,1)S(1)}, bf16[2,736,128]{2,1,0:T(8,128)(2,1)S(1)}, u32[]{:S(2)}, u32[]{:S(2)}) collective-permute-start(bf16[2,736,128]{2,1,0:T(8,128)(2,1)S(1)} %get-tuple-element.204), channel_id=1, source_target_pairs={{0,4},{4,0},{8,12},{12,8},{16,20},{20,16},{24,28},{28,24},{1,5},{5... | collective-permute-start | bytes 1130504 | tf_op jit(solution)/shard_map/ppermute | solution.py:769
  286.0 11.8 %collective-permute-start.30 = (bf16[2,736,128]{2,1,0:T(8,128)(2,1)S(1)}, bf16[2,736,128]{2,1,0:T(8,128)(2,1)S(1)}, u32[]{:S(2)}, u32[]{:S(2)}) collective-permute-start(bf16[2,736,128]{2,1,0:T(8,128)(2,1)S(1)} %get-tuple-element.208), channel_id=1, source_target_pairs={{0,2},{1,3},{2,0},{3,1},{4,6},{5,7},{6,4},{7,5},{8,10},{9,11},{10,... | collective-permute-start | bytes 1130504 | tf_op jit(solution)/shard_map/ppermute | solution.py:769
  286.4 15.8 %collective-permute-start.33 = (f32[2,9,384]{2,1,0:T(8,128)S(1)}, f32[2,9,384]{2,1,0:T(8,128)S(1)}, u32[]{:S(2)}, u32[]{:S(2)}) collective-permute-start(f32[2,9,384]{2,1,0:T(8,128)S(1)} %pad_maximum_fusion.1), channel_id=1, source_target_pairs={{0,1},{1,0},{2,3},{3,2},{4,5},{5,4},{6,7},{7,6},{8,9},{9,8},{10,11... | collective-permute-start | bytes 82952 | tf_op jit(solution)/shard_map/ppermute | solution.py:769
  286.4 17.6 %collective-permute-start.22 = (bf16[2,736,128]{2,1,0:T(8,128)(2,1)S(1)}, bf16[2,736,128]{2,1,0:T(8,128)(2,1)S(1)}, u32[]{:S(2)}, u32[]{:S(2)}) collective-permute-start(bf16[2,736,128]{2,1,0:T(8,128)(2,1)S(1)} %get-tuple-element.203), channel_id=1, source_target_pairs={{0,2},{1,3},{2,0},{3,1},{4,6},{5,7},{6,4},{7,5},{8,10},{9,11},{10,... | collective-permute-start | bytes 1130504 | tf_op jit(solution)/shard_map/ppermute | solution.py:769
  288.1 12.3 %collective-permute-start.31 = (bf16[2,736,128]{2,1,0:T(8,128)(2,1)S(1)}, bf16[2,736,128]{2,1,0:T(8,128)(2,1)S(1)}, u32[]{:S(2)}, u32[]{:S(2)}) collective-permute-start(bf16[2,736,128]{2,1,0:T(8,128)(2,1)S(1)} %get-tuple-element.207), channel_id=1, source_target_pairs={{0,4},{4,0},{8,12},{12,8},{16,20},{20,16},{24,28},{28,24},{1,5},{5... | collective-permute-start | bytes 1130504 | tf_op jit(solution)/shard_map/ppermute | solution.py:769
  293.2 10.8 %collective-permute-start.25 = (bf16[2,736,128]{2,1,0:T(8,128)(2,1)S(1)}, bf16[2,736,128]{2,1,0:T(8,128)(2,1)S(1)}, u32[]{:S(2)}, u32[]{:S(2)}) collective-permute-start(bf16[2,736,128]{2,1,0:T(8,128)(2,1)S(1)} %fusion.11), channel_id=1, source_target_pairs={{0,8},{4,12},{8,0},{12,4},{16,24},{20,28},{24,16},{28,20},{1,9},{5... | collective-permute-start | bytes 1130504 | tf_op jit(solution)/shard_map/ppermute | solution.py:769
  300.6 14.2 %collective-permute-start.32 = (bf16[2,736,128]{2,1,0:T(8,128)(2,1)S(1)}, bf16[2,736,128]{2,1,0:T(8,128)(2,1)S(1)}, u32[]{:S(2)}, u32[]{:S(2)}) collective-permute-start(bf16[2,736,128]{2,1,0:T(8,128)(2,1)S(1)} %fusion.7), channel_id=1, source_target_pairs={{0,8},{4,12},{8,0},{12,4},{16,24},{20,28},{24,16},{28,20},{1,9},{5... | collective-permute-start | bytes 1130504 | tf_op jit(solution)/shard_map/ppermute | solution.py:769
  304.3 29.8 %collective-permute-start.26 = (bf16[1,736,128]{2,1,0:T(8,128)(2,1)S(1)}, bf16[1,736,128]{2,1,0:T(8,128)(2,1)S(1)}, u32[]{:S(2)}, u32[]{:S(2)}) collective-permute-start(bf16[1,736,128]{2,1,0:T(8,128)(2,1)S(1)} %slice.278), channel_id=1, source_target_pairs={{0,16},{4,20},{8,24},{12,28},{16,0},{20,4},{24,8},{28,12},{1,17},{... | collective-permute-start | bytes 565256 | tf_op jit(solution)/shard_map/ppermute | solution.py:769
  (40 other events, 343.8 us)
